TPU v7x, 128 devices: a whole 4x4x4 slice. The times are simulated.
128 devices in a mesh: dp: 8 (over y, x_hi), ctx: 16 (over x_lo, z, core).
Axes of the slice: x: 4 (x_hi: 2, x_lo: 2; x = x_hi * 2 + x_lo), y: 4, z: 4, core: 2. Of those that a mesh axis runs over, the one named last changes fastest.
Arguments:
- teacher_query: bfloat16 [8, 2048, 2048], P('dp', 'ctx'), may hold values from -20 to 20
- teacher_key: bfloat16 [8, 2048, 2048], P('dp', 'ctx'), may hold values from -20 to 20
- student_hidden: bfloat16 [8, 2048, 1536], P('dp', 'ctx'), may hold values from -20 to 20
- weight_query: bfloat16 [1536, 768], replicated, may hold values from -0.15625 to 0.15625
- weight_key: bfloat16 [1536, 768], replicated, may hold values from -0.15625 to 0.15625
- doc_lengths: int32 [8, 8], P('dp'), may hold values from 1 to 256, as said below
Outputs:
- group_loss: float32 [8], P('dp')
- grad_hidden: bfloat16 [8, 2048, 1536], P('dp', 'ctx')
- grad_wq: float32 [1536, 768], P('ctx')
- grad_wk: float32 [1536, 768], P('ctx')
Inputs may be any that keep to these rules, and one draw needn't show every extreme that they name: `doc_lengths`: each group's 8 lengths are positive and sum to 1984 (the positions after them are padding); the last document is the longest, exactly 256.
All inputs are finite; a program needn't handle non-finite values.
Results may differ from a plain program's by a relative error of at most 0.015.
The roundings to bfloat16 on the way count: a program that leaves them out, or rounds other values in their place, can miss the bound.
Values may be sent and summed in bfloat16 or wider, within the bound.
A program may use at most 128 MiB of HBM per device.

v0:
```python
import math

import jax
import jax.numpy as jnp
from jax import lax
from jax.sharding import PartitionSpec as P

TDH = 128
SDH = 48
DOCS = 8


loss_scale = 1048576.0
negative_big = -1e30


def shifted(value, axis, steps):
    count = lax.axis_size(axis)
    first, last = (max(0, -steps), min(count, count - steps))
    return lax.ppermute(value, axis, [(source, source + steps) for source in range(first, last)])


def document_ids(positions, bounds):
    return jnp.sum((positions[:, None] >= bounds[None, :]).astype(jnp.int32), axis=1)


def online_update(highest, summed, scores, allowed):
    block_high = jnp.max(jnp.where(allowed, scores, negative_big), axis=2)
    new_high = jnp.maximum(highest, block_high)
    new_sum = summed * jnp.exp(highest - new_high) + jnp.sum(
        jnp.where(allowed, jnp.exp(scores - new_high[:, :, None]), 0.0), axis=2
    )
    return (new_high, new_sum)


def row_statistics(
    teacher_rows, student_rows, teacher_keys, student_keys, key_docs, row_docs, block_size
):
    row_count = teacher_rows.shape[0]
    head_count = teacher_rows.shape[1] // TDH
    teacher_here = teacher_rows.reshape(row_count, head_count, TDH)
    student_here = student_rows.reshape(row_count, head_count, SDH)
    block_count = teacher_keys.shape[0] // block_size
    teacher_blocks = teacher_keys.reshape(block_count, block_size, head_count, TDH)
    student_blocks = student_keys.reshape(block_count, block_size, head_count, SDH)
    doc_blocks = key_docs.reshape(block_count, block_size)
    row_valid = row_docs < DOCS

    def row_advance(running, block):
        teacher_block, student_block, doc_block = block
        allowed = ((row_docs[:, None] == doc_block[None, :]) & row_valid[:, None])[None]
        teacher_scores = jnp.einsum(
            "rhd,khd->hrk", teacher_here, teacher_block, preferred_element_type=jnp.float32
        ) * (1.0 / math.sqrt(TDH))
        student_scores = jnp.einsum(
            "rhd,khd->hrk", student_here, student_block, preferred_element_type=jnp.float32
        ) * (1.0 / math.sqrt(SDH))
        teacher_high, teacher_sum = online_update(running[0], running[1], teacher_scores, allowed)
        student_high, student_sum = online_update(running[2], running[3], student_scores, allowed)
        return ((teacher_high, teacher_sum, student_high, student_sum), None)

    start_high = jnp.full((head_count, row_count), negative_big, jnp.float32)
    start_sum = jnp.zeros((head_count, row_count), jnp.float32)
    final, _ = lax.scan(
        row_advance,
        (start_high, start_sum, start_high, start_sum),
        (teacher_blocks, student_blocks, doc_blocks),
    )
    valid_rows = row_valid[None, :]
    teacher_total = jnp.where(
        valid_rows, final[0] + jnp.log(jnp.where(valid_rows, final[1], 1.0)), 0.0
    )
    student_total = jnp.where(
        valid_rows, final[2] + jnp.log(jnp.where(valid_rows, final[3], 1.0)), 0.0
    )
    return (teacher_total, student_total)


def relation_gradient(
    teacher_rows,
    student_rows,
    teacher_keys,
    student_keys,
    key_docs,
    row_docs,
    row_totals,
    key_totals,
    coefficient,
    block_size,
):
    row_count = teacher_rows.shape[0]
    head_count = teacher_rows.shape[1] // TDH
    teacher_here = teacher_rows.reshape(row_count, head_count, TDH)
    student_here = student_rows.reshape(row_count, head_count, SDH)
    block_count = teacher_keys.shape[0] // block_size
    teacher_blocks = teacher_keys.reshape(block_count, block_size, head_count, TDH)
    student_blocks = student_keys.reshape(block_count, block_size, head_count, SDH)
    doc_blocks = key_docs.reshape(block_count, block_size)
    teacher_key_blocks = (
        key_totals[0].reshape(head_count, block_count, block_size).transpose(1, 0, 2)
    )
    student_key_blocks = (
        key_totals[1].reshape(head_count, block_count, block_size).transpose(1, 0, 2)
    )
    teacher_total = row_totals[0][:, :, None]
    student_total = row_totals[1][:, :, None]
    row_valid = row_docs < DOCS

    def relation_advance(running, block):
        teacher_block, student_block, doc_block, teacher_key_total, student_key_total = block
        allowed = ((row_docs[:, None] == doc_block[None, :]) & row_valid[:, None])[None]
        teacher_scores = jnp.einsum(
            "rhd,khd->hrk", teacher_here, teacher_block, preferred_element_type=jnp.float32
        ) * (1.0 / math.sqrt(TDH))
        student_scores = jnp.einsum(
            "rhd,khd->hrk", student_here, student_block, preferred_element_type=jnp.float32
        ) * (1.0 / math.sqrt(SDH))
        teacher_prob = jnp.where(allowed, jnp.exp(teacher_scores - teacher_total), 0.0)
        student_prob = jnp.where(allowed, jnp.exp(student_scores - student_total), 0.0)
        teacher_back = jnp.where(
            allowed, jnp.exp(teacher_scores - teacher_key_total[:, None, :]), 0.0
        )
        student_back = jnp.where(
            allowed, jnp.exp(student_scores - student_key_total[:, None, :]), 0.0
        )
        weights = (
            coefficient * (student_prob - teacher_prob + (student_back - teacher_back))
        ).astype(jnp.bfloat16)
        grad_block = jnp.einsum(
            "hrk,khd->rhd", weights, student_block, preferred_element_type=jnp.float32
        ) * (1.0 / math.sqrt(SDH))
        divergence = jnp.sum(
            jnp.where(
                allowed,
                teacher_prob * (teacher_scores - teacher_total - (student_scores - student_total)),
                0.0,
            )
        )
        return ((running[0] + grad_block, running[1] + divergence), None)

    start = (jnp.zeros((row_count, head_count, SDH), jnp.float32), jnp.zeros((), jnp.float32))
    final, _ = lax.scan(
        relation_advance,
        start,
        (teacher_blocks, student_blocks, doc_blocks, teacher_key_blocks, student_key_blocks),
    )
    return (final[0].reshape(row_count, head_count * SDH), final[1])


def per_device(teacher_query, teacher_key, student_hidden, weight_query, weight_key, doc_lengths):
    cycle_size = lax.axis_size("ctx")
    cycle_index = lax.axis_index("ctx")
    hidden_rows = student_hidden[0]
    teacher_queries = teacher_query[0]
    teacher_keys = teacher_key[0]
    row_count = hidden_rows.shape[0]
    teacher_width = teacher_queries.shape[1]
    head_count = teacher_width // TDH
    student_queries = jnp.dot(hidden_rows, weight_query, preferred_element_type=jnp.float32).astype(
        jnp.bfloat16
    )
    student_keys = jnp.dot(hidden_rows, weight_key, preferred_element_type=jnp.float32).astype(
        jnp.bfloat16
    )
    student_width = student_queries.shape[1]
    bounds = jnp.cumsum(doc_lengths[0])
    valid_count = jnp.sum(doc_lengths[0]).astype(jnp.float32)
    coefficient = loss_scale / (head_count * valid_count)
    local_order = jnp.arange(row_count, dtype=jnp.int32)
    row_positions = cycle_index * row_count + local_order
    row_docs = document_ids(row_positions, bounds)
    local_blocks = jnp.concatenate(
        [teacher_queries, teacher_keys, student_queries, student_keys], axis=1
    )
    seq_length = row_count * cycle_size
    offsets = []
    reach_blocks = (seq_length // 8 + row_count - 2) // row_count
    offsets = [offset for offset in range(-reach_blocks, reach_blocks + 1) if offset != 0]
    pieces = [local_blocks]
    position_parts = [row_positions]
    for offset in offsets:
        pieces.append(shifted(local_blocks, "ctx", offset))
        source = cycle_index - offset
        inside = (source >= 0) & (source < cycle_size)
        position_parts.append(jnp.where(inside, source * row_count + local_order, -1))
    gathered = jnp.concatenate(pieces, axis=0)
    key_positions = jnp.concatenate(position_parts, axis=0)
    key_docs = jnp.where(key_positions >= 0, document_ids(key_positions, bounds), DOCS + 1)
    key_total = gathered.shape[0]
    block_size = row_count * max(1, 512 // row_count)
    padded_total = (key_total + block_size - 1) // block_size * block_size
    extra_rows = padded_total - key_total
    gathered = jnp.pad(gathered, ((0, extra_rows), (0, 0)))
    key_docs = jnp.pad(key_docs, (0, extra_rows), constant_values=DOCS + 1)
    keys_teacher_q = gathered[:, :teacher_width]
    keys_teacher_k = gathered[:, teacher_width : 2 * teacher_width]
    keys_student_q = gathered[:, 2 * teacher_width : 2 * teacher_width + student_width]
    keys_student_k = gathered[:, 2 * teacher_width + student_width :]
    query_teacher_total, query_student_total = row_statistics(
        teacher_queries,
        student_queries,
        keys_teacher_q,
        keys_student_q,
        key_docs,
        row_docs,
        block_size,
    )
    key_teacher_total, key_student_total = row_statistics(
        teacher_keys, student_keys, keys_teacher_k, keys_student_k, key_docs, row_docs, block_size
    )
    stacked = jnp.stack(
        [query_teacher_total, query_student_total, key_teacher_total, key_student_total]
    )
    total_parts = [stacked]
    for offset in offsets:
        total_parts.append(shifted(stacked, "ctx", offset))
    far_totals = jnp.concatenate(total_parts, axis=2)
    far_totals = jnp.pad(far_totals, ((0, 0), (0, 0), (0, extra_rows)))
    grad_queries, divergence_q = relation_gradient(
        teacher_queries,
        student_queries,
        keys_teacher_q,
        keys_student_q,
        key_docs,
        row_docs,
        (query_teacher_total, query_student_total),
        (far_totals[0], far_totals[1]),
        coefficient,
        block_size,
    )
    grad_keys, divergence_k = relation_gradient(
        teacher_keys,
        student_keys,
        keys_teacher_k,
        keys_student_k,
        key_docs,
        row_docs,
        (key_teacher_total, key_student_total),
        (far_totals[2], far_totals[3]),
        coefficient,
        block_size,
    )
    query_grad_b = grad_queries.astype(jnp.bfloat16)
    key_grad_b = grad_keys.astype(jnp.bfloat16)
    hidden_grad = (
        jnp.dot(query_grad_b, weight_query.T, preferred_element_type=jnp.float32)
        + jnp.dot(key_grad_b, weight_key.T, preferred_element_type=jnp.float32)
    ).astype(jnp.bfloat16)
    both_grads = jnp.concatenate([query_grad_b, key_grad_b], axis=1)
    shard_rows = hidden_rows.shape[1] // cycle_size
    local_terms = lax.dot_general(
        hidden_rows, both_grads, (((0,), (0,)), ((), ())), preferred_element_type=jnp.float32
    )
    summed = lax.psum(local_terms, ("dp", "ctx"))
    own_rows = lax.dynamic_slice_in_dim(summed, cycle_index * shard_rows, shard_rows, 0)
    divergence_total = lax.psum(divergence_q + divergence_k, "ctx")
    group_value = (divergence_total / (head_count * valid_count)).reshape(1)
    return (
        group_value,
        hidden_grad[None],
        own_rows[:, :student_width],
        own_rows[:, student_width:],
    )


def solution(mesh):
    in_specs = (
        P("dp", "ctx", None),
        P("dp", "ctx", None),
        P("dp", "ctx", None),
        P(),
        P(),
        P("dp", None),
    )
    out_specs = (P("dp"), P("dp", "ctx", None), P("ctx", None), P("ctx", None))
    return jax.shard_map(
        per_device, mesh=mesh, in_specs=in_specs, out_specs=out_specs, check_vma=False
    )
```

profile of v0, /device:TPU:1, one launch (start us, length us, event | category | flops | bytes accessed | tf_op | source)
XLA Modules:
  0.0 423.8 jit_solution(8254641078359232006)
XLA Ops:
  17.6 4.2 collective-permute-start.2
  21.8 4.8 %collective-permute-start.3 = (bf16[128,5632]{1,0:T(8,128)(2,1)}, bf16[128,5632]{1,0:T(8,128)(2,1)}, u32[]{:S(2)}, u32[]{:S(2)}) collective-permute-start(bf16[128,5632]{1,0:T(8,128)(2,1)} %get-tuple-element.786), channel_id=1, source_target_pairs={{0,2},{1,3},{2,4},{3,5},{4,6},{5,7},{6,8},{7,9},{8,10},{9,11},{10,... | collective-permute-start | bytes 4325384 | tf_op jit(solution)/shard_map/ppermute | solution.py:20
  33.9 15.1 %collective-permute-done = bf16[128,5632]{1,0:T(8,128)(2,1)} collective-permute-done((bf16[128,5632]{1,0:T(8,128)(2,1)}, bf16[128,5632]{1,0:T(8,128)(2,1)}, u32[]{:S(2)}, u32[]{:S(2)}) %collective-permute-start) | collective-permute-done | bytes 1441824 | tf_op jit(solution)/shard_map/ppermute | solution.py:20
  51.5 13.5 %collective-permute-done.1 = bf16[128,5632]{1,0:T(8,128)(2,1)} collective-permute-done((bf16[128,5632]{1,0:T(8,128)(2,1)}, bf16[128,5632]{1,0:T(8,128)(2,1)}, u32[]{:S(2)}, u32[]{:S(2)}) %collective-permute-start.1) | collective-permute-done | bytes 1441824 | tf_op jit(solution)/shard_map/ppermute | solution.py:20
  72.8 5.1 %fusion.101 = (bf16[128,8,16,128]{3,1,2,0:T(8,128)(2,1)}, bf16[128,8,16,128]{3,1,2,0:T(8,128)(2,1)S(1)}) fusion(bf16[640,5632]{1,0:T(8,128)(2,1)} %constant_dynamic-update-slice_fusion), kind=kLoop, calls=%fused_computation.132 | loop fusion | bytes 15597568
  87.9 3.9 reshape.249
  94.6 22.8 %while.60 = (s32[]{:T(128)}, f32[16,128]{1,0:T(8,128)S(1)}, f32[16,128]{1,0:T(8,128)S(1)}, f32[16,128]{1,0:T(8,128)S(1)}, f32[16,128]{1,0:T(8,128)S(1)}, /*index...) while((s32[]{:T(128)}, f32[16,128]{1,0:T(8,128)S(1)}, ...), condition=%wide.region_8.9_spmd.clone, body=%wide.region_3.8_spmd.clone.sunk | while | flops 383930368 | bytes 48061772 | solution.py:64
  97.2 3.5 fusion.169
  100.7 5.2 %fusion.170 = (f32[16,128]{1,0:T(8,128)S(1)}, f32[16,128]{1,0:T(8,128)S(1)}) fusion(f32[16,512,128]{2,1,0:T(8,128)} %get-tuple-element.1119, f32[16,128]{1,0:T(8,128)S(1)} %select_maximum_fusion.9, pred[128,512]{0,1:T(8,128)(4,1)S(1)} %compare_and_fusion.8, f32[16,128]{1,0:T(8,128)S(1)} %select_maximum_fusion.8, f32[16,512,128]{2,1,0:T(8,128)} %copy-done.1), kind=kLoop, calls=%fused_computation.5.clone.1 | loop fusion | flops 8384512 | bytes 8486912 | tf_op jit(solution)/shard_map/while/body/eval_jaxpr/reduce_sum | solution.py:30
  108.6 3.5 fusion.169
  112.1 5.2 %fusion.170 = (f32[16,128]{1,0:T(8,128)S(1)}, f32[16,128]{1,0:T(8,128)S(1)}) fusion(f32[16,512,128]{2,1,0:T(8,128)} %get-tuple-element.1119, f32[16,128]{1,0:T(8,128)S(1)} %select_maximum_fusion.9, pred[128,512]{0,1:T(8,128)(4,1)S(1)} %compare_and_fusion.8, f32[16,128]{1,0:T(8,128)S(1)} %select_maximum_fusion.8, f32[16,512,128]{2,1,0:T(8,128)} %copy-done.1), kind=kLoop, calls=%fused_computation.5.clone.1 | loop fusion | flops 8384512 | bytes 8486912 | tf_op jit(solution)/shard_map/while/body/eval_jaxpr/reduce_sum | solution.py:30
  117.4 3.6 copy.77
  126.7 3.9 reshape.256
  133.5 22.7 %while.61 = (s32[]{:T(128)}, f32[16,128]{1,0:T(8,128)S(1)}, f32[16,128]{1,0:T(8,128)S(1)}, f32[16,128]{1,0:T(8,128)S(1)}, f32[16,128]{1,0:T(8,128)S(1)}, /*index...) while((s32[]{:T(128)}, f32[16,128]{1,0:T(8,128)S(1)}, ...), condition=%wide.region_14.15_spmd.clone, body=%wide.region_9.14_spmd.clone.sunk | while | flops 383930368 | bytes 48061772 | solution.py:64
  136.1 3.4 fusion.176
  139.5 5.2 %fusion.177 = (f32[16,128]{1,0:T(8,128)S(1)}, f32[16,128]{1,0:T(8,128)S(1)}) fusion(f32[16,512,128]{2,1,0:T(8,128)} %get-tuple-element.1138, f32[16,128]{1,0:T(8,128)S(1)} %select_maximum_fusion.11, pred[128,512]{0,1:T(8,128)(4,1)S(1)} %compare_and_fusion.9, f32[16,128]{1,0:T(8,128)S(1)} %select_maximum_fusion.10, f32[16,512,128]{2,1,0:T(8,128)} %copy-done.2), kind=kLoop, calls=%fused_computation.33.clone.1 | loop fusion | flops 8384512 | bytes 8486912 | tf_op jit(solution)/shard_map/while/body/eval_jaxpr/reduce_sum | solution.py:30
  150.9 5.2 %fusion.177 = (f32[16,128]{1,0:T(8,128)S(1)}, f32[16,128]{1,0:T(8,128)S(1)}) fusion(f32[16,512,128]{2,1,0:T(8,128)} %get-tuple-element.1138, f32[16,128]{1,0:T(8,128)S(1)} %select_maximum_fusion.11, pred[128,512]{0,1:T(8,128)(4,1)S(1)} %compare_and_fusion.9, f32[16,128]{1,0:T(8,128)S(1)} %select_maximum_fusion.10, f32[16,512,128]{2,1,0:T(8,128)} %copy-done.2), kind=kLoop, calls=%fused_computation.33.clone.1 | loop fusion | flops 8384512 | bytes 8486912 | tf_op jit(solution)/shard_map/while/body/eval_jaxpr/reduce_sum | solution.py:30
  162.0 3.6 collective-permute-start.6
  165.7 4.2 collective-permute-start.7
  174.0 29.6 %while.63 = (s32[]{:T(128)}, f32[128,16,48]{0,2,1:T(8,128)}, f32[]{:T(128)}, bf16[2,512,16,48]{1,3,2,0:T(8,128)(2,1)}, f32[]{:T(128)}, /*index=5*/s32[128]{0:T(1...) while((s32[]{:T(128)}, f32[128,16,48]{0,2,1:T(8,128)}, ...), condition=%wide.region_21.22_spmd.clone, body=%wide.region_19.21_spmd.clone.sunk | while | flops 495353856 | bytes 62431692 | solution.py:142
  176.5 4.2 fusion.193
  180.9 7.2 %fusion.194 = f32[128,16,48]{0,2,1:T(8,128)} fusion(f32[16,512,128]{2,1,0:T(8,128)} %get-tuple-element.1178, f32[16,512,128]{2,1,0:T(8,128)} %copy-done.3, f32[16,512]{1,0:T(8,128)S(1)} %bitcast.404, f32[16,512]{1,0:T(8,128)S(1)} %bitcast.405, f32[16,128]{1,0:T(8,128)} %bitcast.418, f32[16,128]{1,0:T(8,128)} %bitcast.420, f32[]{:T(128)} %get-tuple-element.1355, ...), kind=kOutput, calls=%fused_computation.108.clone.1 | convolution fusion | flops 116686848 | bytes 10109953 | tf_op jit(solution)/shard_map/while/body/eval_jaxpr/hrk,khd->rhd/dot_general | solution.py:129
  191.2 4.2 %fusion.193 = (f32[]{:T(128)}, f32[16,512,128]{2,1,0:T(8,128)}) fusion(f32[16,512,128]{2,1,0:T(8,128)S(1)} %fusion.192, f32[16,128]{1,0:T(8,128)S(1)} %bitcast.419, f32[16,128]{1,0:T(8,128)S(1)} %bitcast.421, pred[128,512]{0,1:T(8,128)(4,1)S(1)} %compare_and_fusion.11, bf16[128,16,128]{2,0,1:T(8,128)(2,1)S(1)} %copy-done.10, ...), kind=kOutput, calls=%fused_computation.92.clone.1 | convolution fusion | flops 277872640 | bytes 11091976 | tf_op jit(solution)/shard_map/while/body/eval_jaxpr/rhd,khd->hrk/dot_general | solution.py:112
  195.6 7.3 %fusion.194 = f32[128,16,48]{0,2,1:T(8,128)} fusion(f32[16,512,128]{2,1,0:T(8,128)} %get-tuple-element.1178, f32[16,512,128]{2,1,0:T(8,128)} %copy-done.3, f32[16,512]{1,0:T(8,128)S(1)} %bitcast.404, f32[16,512]{1,0:T(8,128)S(1)} %bitcast.405, f32[16,128]{1,0:T(8,128)} %bitcast.418, f32[16,128]{1,0:T(8,128)} %bitcast.420, f32[]{:T(128)} %get-tuple-element.1355, ...), kind=kOutput, calls=%fused_computation.108.clone.1 | convolution fusion | flops 116686848 | bytes 10109953 | tf_op jit(solution)/shard_map/while/body/eval_jaxpr/hrk,khd->rhd/dot_general | solution.py:129
  206.4 29.2 %while.62 = (s32[]{:T(128)}, f32[128,16,48]{0,2,1:T(8,128)}, f32[]{:T(128)}, bf16[2,512,16,48]{1,3,2,0:T(8,128)(2,1)}, f32[]{:T(128)}, /*index=5*/s32[128]{0:T(1...) while((s32[]{:T(128)}, f32[128,16,48]{0,2,1:T(8,128)}, ...), condition=%wide.region_18.19_spmd.clone, body=%wide.region_16.18_spmd.clone.sunk | while | flops 495353856 | bytes 60203440 | solution.py:142
  208.9 4.3 %fusion.185 = (f32[]{:T(128)}, f32[16,512,128]{2,1,0:T(8,128)}) fusion(f32[16,512,128]{2,1,0:T(8,128)S(1)} %fusion.184, f32[16,128]{1,0:T(8,128)S(1)} %bitcast.415, f32[16,128]{1,0:T(8,128)S(1)} %bitcast.417, pred[128,512]{0,1:T(8,128)(4,1)S(1)} %compare_and_fusion.10, bf16[128,16,128]{2,0,1:T(8,128)(2,1)S(1)} %get-tuple-element.1311, ...), kind=kOutput, calls=%fused_computation.58.clone.1 | convolution fusion | flops 277872640 | bytes 11091976 | tf_op jit(solution)/shard_map/while/body/eval_jaxpr/rhd,khd->hrk/dot_general | solution.py:112
  213.1 7.2 %fusion.186 = f32[128,16,48]{0,2,1:T(8,128)} fusion(f32[16,512,128]{2,1,0:T(8,128)} %get-tuple-element.1159, f32[16,512,128]{2,1,0:T(8,128)} %copy-done.4, f32[16,512]{1,0:T(8,128)S(1)} %get-tuple-element.1160, f32[16,512]{1,0:T(8,128)S(1)} %get-tuple-element.1161, f32[16,128]{1,0:T(8,128)} %bitcast.414, f32[16,128]{1,0:T(8,128)} %bitcast.416, ...), kind=kOutput, calls=%fused_computation.74.clone.1 | convolution fusion | flops 116686848 | bytes 10109953 | tf_op jit(solution)/shard_map/while/body/eval_jaxpr/hrk,khd->rhd/dot_general | solution.py:129
  223.4 4.3 %fusion.185 = (f32[]{:T(128)}, f32[16,512,128]{2,1,0:T(8,128)}) fusion(f32[16,512,128]{2,1,0:T(8,128)S(1)} %fusion.184, f32[16,128]{1,0:T(8,128)S(1)} %bitcast.415, f32[16,128]{1,0:T(8,128)S(1)} %bitcast.417, pred[128,512]{0,1:T(8,128)(4,1)S(1)} %compare_and_fusion.10, bf16[128,16,128]{2,0,1:T(8,128)(2,1)S(1)} %get-tuple-element.1311, ...), kind=kOutput, calls=%fused_computation.58.clone.1 | convolution fusion | flops 277872640 | bytes 11091976 | tf_op jit(solution)/shard_map/while/body/eval_jaxpr/rhd,khd->hrk/dot_general | solution.py:112
  227.7 7.3 %fusion.186 = f32[128,16,48]{0,2,1:T(8,128)} fusion(f32[16,512,128]{2,1,0:T(8,128)} %get-tuple-element.1159, f32[16,512,128]{2,1,0:T(8,128)} %copy-done.4, f32[16,512]{1,0:T(8,128)S(1)} %get-tuple-element.1160, f32[16,512]{1,0:T(8,128)S(1)} %get-tuple-element.1161, f32[16,128]{1,0:T(8,128)} %bitcast.414, f32[16,128]{1,0:T(8,128)} %bitcast.416, ...), kind=kOutput, calls=%fused_computation.74.clone.1 | convolution fusion | flops 116686848 | bytes 10109953 | tf_op jit(solution)/shard_map/while/body/eval_jaxpr/hrk,khd->rhd/dot_general | solution.py:129
  236.6 6.0 %convolution_bitcast_fusion = f32[1536,1536]{0,1:T(8,128)} fusion(bf16[128,768]{0,1:T(8,128)(2,1)S(1)} %bitcast.400, bf16[128,768]{0,1:T(8,128)(2,1)S(1)} %bitcast.402, bf16[1,128,1536]{2,1,0:T(8,128)(2,1)} %param.16), kind=kOutput, calls=%fused_computation.130 | convolution fusion | flops 604766208 | bytes 10223616 | tf_op jit(solution)/shard_map/dot_general | solution.py:251
  242.6 30.7 %psum.14 = f32[]{:T(128)} all-reduce(f32[]{:T(128)S(6)} %add.125), channel_id=1, replica_groups=mesh['dp'=8,'ctx'=16] {'ctx'}, use_global_device_ids=true, to_apply=%region_22.23 | all-reduce | flops 1 | bytes 8 | tf_op jit(solution)/shard_map/psum | solution.py:256
  277.3 135.1 %all-reduce.5.cloned.1.call-done = f32[1536,1536]{0,1:T(8,128)} async-done(((f32[1536,1536]{0,1:T(8,128)}), f32[1536,1536]{0,1:T(8,128)}) %all-reduce.5.cloned.1.call-update) | async-done | bytes 9437200 | tf_op jit(solution)/shard_map/psum | solution.py:254
  (194 shorter events, 93.0 us)
Async XLA Ops:
  7.2 2.5 copy-start
  7.2 4.0 copy-start.12
  7.2 405.2 %all-reduce.5.cloned.1.call-start = ((), (), s32[]{:S(2)}) async-start(), calls=%async_computation | async-start | bytes 18874368 | tf_op jit(solution)/shard_map/psum | solution.py:254
  7.2 4.0 copy-start.13
  9.7 17.0 %copy-start.18 = (s32[1,8]{1,0:T(1,128)S(1)}, s32[1,8]{1,0:T(1,128)}, u32[]{:S(2)}) copy-start(s32[1,8]{1,0:T(1,128)} %param.19) | copy-start | bytes 100
  13.0 35.9 %collective-permute-start = (bf16[128,5632]{1,0:T(8,128)(2,1)}, bf16[128,5632]{1,0:T(8,128)(2,1)}, u32[]{:S(2)}, u32[]{:S(2)}) collective-permute-start(bf16[128,5632]{1,0:T(8,128)(2,1)} %get-tuple-element.786), channel_id=1, source_target_pairs={{2,0},{3,1},{4,2},{5,3},{6,4},{7,5},{8,6},{9,7},{10,8},{11,9},{12,... | collective-permute-start | bytes 4325384 | tf_op jit(solution)/shard_map/ppermute | solution.py:20
  14.3 50.7 %collective-permute-start.1 = (bf16[128,5632]{1,0:T(8,128)(2,1)}, bf16[128,5632]{1,0:T(8,128)(2,1)}, u32[]{:S(2)}, u32[]{:S(2)}) collective-permute-start(bf16[128,5632]{1,0:T(8,128)(2,1)} %get-tuple-element.786), channel_id=1, source_target_pairs={{1,0},{2,1},{3,2},{4,3},{5,4},{6,5},{7,6},{8,7},{9,8},{10,9},{11,1... | collective-permute-start | bytes 4325384 | tf_op jit(solution)/shard_map/ppermute | solution.py:20
  17.6 49.9 %collective-permute-start.2 = (bf16[128,5632]{1,0:T(8,128)(2,1)}, bf16[128,5632]{1,0:T(8,128)(2,1)}, u32[]{:S(2)}, u32[]{:S(2)}) collective-permute-start(bf16[128,5632]{1,0:T(8,128)(2,1)} %get-tuple-element.786), channel_id=1, source_target_pairs={{0,1},{1,2},{2,3},{3,4},{4,5},{5,6},{6,7},{7,8},{8,9},{9,10},{10,1... | collective-permute-start | bytes 4325384 | tf_op jit(solution)/shard_map/ppermute | solution.py:20
  21.8 48.3 %collective-permute-start.3 = (bf16[128,5632]{1,0:T(8,128)(2,1)}, bf16[128,5632]{1,0:T(8,128)(2,1)}, u32[]{:S(2)}, u32[]{:S(2)}) collective-permute-start(bf16[128,5632]{1,0:T(8,128)(2,1)} %get-tuple-element.786), channel_id=1, source_target_pairs={{0,2},{1,3},{2,4},{3,5},{4,6},{5,7},{6,8},{7,9},{8,10},{9,11},{10,... | collective-permute-start | bytes 4325384 | tf_op jit(solution)/shard_map/ppermute | solution.py:20
  72.8 6.2 %copy-start.9 = (bf16[640,5632]{1,0:T(8,128)(2,1)S(1)}, bf16[640,5632]{1,0:T(8,128)(2,1)}, u32[]{:S(2)}) copy-start(bf16[640,5632]{1,0:T(8,128)(2,1)} %constant_dynamic-update-slice_fusion) | copy-start | bytes 21626884
  94.6 2.6 copy-start.5
  97.2 3.5 copy-start.1
  106.0 2.6 copy-start.5
  108.6 3.5 copy-start.1
  133.5 2.6 copy-start.6
  136.1 3.5 copy-start.2
  144.8 2.7 copy-start.6
  147.5 3.5 copy-start.2
  157.5 12.4 %collective-permute-start.4 = (f32[4,16,128]{2,1,0:T(8,128)S(1)}, f32[4,16,128]{2,1,0:T(8,128)S(1)}, u32[]{:S(2)}, u32[]{:S(2)}) collective-permute-start(f32[4,16,128]{2,1,0:T(8,128)S(1)} %get-tuple-element.792), channel_id=1, source_target_pairs={{2,0},{3,1},{4,2},{5,3},{6,4},{7,5},{8,6},{9,7},{10,8},{11,9},{12,... | collective-permute-start | bytes 98312 | tf_op jit(solution)/shard_map/ppermute | solution.py:20
  160.1 10.4 %collective-permute-start.5 = (f32[4,16,128]{2,1,0:T(8,128)S(1)}, f32[4,16,128]{2,1,0:T(8,128)S(1)}, u32[]{:S(2)}, u32[]{:S(2)}) collective-permute-start(f32[4,16,128]{2,1,0:T(8,128)S(1)} %get-tuple-element.792), channel_id=1, source_target_pairs={{1,0},{2,1},{3,2},{4,3},{5,4},{6,5},{7,6},{8,7},{9,8},{10,9},{11,1... | collective-permute-start | bytes 98312 | tf_op jit(solution)/shard_map/ppermute | solution.py:20
  162.0 9.1 %collective-permute-start.6 = (f32[4,16,128]{2,1,0:T(8,128)S(1)}, f32[4,16,128]{2,1,0:T(8,128)S(1)}, u32[]{:S(2)}, u32[]{:S(2)}) collective-permute-start(f32[4,16,128]{2,1,0:T(8,128)S(1)} %get-tuple-element.792), channel_id=1, source_target_pairs={{0,1},{1,2},{2,3},{3,4},{4,5},{5,6},{6,7},{7,8},{8,9},{9,10},{10,1... | collective-permute-start | bytes 98312 | tf_op jit(solution)/shard_map/ppermute | solution.py:20
  165.7 6.1 %collective-permute-start.7 = (f32[4,16,128]{2,1,0:T(8,128)S(1)}, f32[4,16,128]{2,1,0:T(8,128)S(1)}, u32[]{:S(2)}, u32[]{:S(2)}) collective-permute-start(f32[4,16,128]{2,1,0:T(8,128)S(1)} %get-tuple-element.792), channel_id=1, source_target_pairs={{0,2},{1,3},{2,4},{3,5},{4,6},{5,7},{6,8},{7,9},{8,10},{9,11},{10,... | collective-permute-start | bytes 98312 | tf_op jit(solution)/shard_map/ppermute | solution.py:20
  174.0 2.5 copy-start.10
  174.0 2.5 copy-start.16
  174.0 2.5 copy-start.17
  176.1 4.7 %copy-start.3 = (f32[16,512,128]{2,1,0:T(8,128)}, f32[16,512,128]{2,1,0:T(8,128)S(1)}, u32[]{:S(2)}) copy-start(f32[16,512,128]{2,1,0:T(8,128)S(1)} %fusion.192) | copy-start | bytes 12582916 | tf_op jit(solution)/shard_map/while
  188.7 2.5 copy-start.10
  188.7 2.5 copy-start.16
  188.7 2.5 copy-start.17
  190.8 4.7 %copy-start.3 = (f32[16,512,128]{2,1,0:T(8,128)}, f32[16,512,128]{2,1,0:T(8,128)S(1)}, u32[]{:S(2)}) copy-start(f32[16,512,128]{2,1,0:T(8,128)S(1)} %fusion.192) | copy-start | bytes 12582916 | tf_op jit(solution)/shard_map/while
  208.5 4.6 %copy-start.4 = (f32[16,512,128]{2,1,0:T(8,128)}, f32[16,512,128]{2,1,0:T(8,128)S(1)}, u32[]{:S(2)}) copy-start(f32[16,512,128]{2,1,0:T(8,128)S(1)} %fusion.184) | copy-start | bytes 12582916 | tf_op jit(solution)/shard_map/while
  223.1 4.6 %copy-start.4 = (f32[16,512,128]{2,1,0:T(8,128)}, f32[16,512,128]{2,1,0:T(8,128)S(1)}, u32[]{:S(2)}) copy-start(f32[16,512,128]{2,1,0:T(8,128)S(1)} %fusion.184) | copy-start | bytes 12582916 | tf_op jit(solution)/shard_map/while
  (9 other events, 21.1 us)
Sparse Core Ops, SparseCore 0:
  242.8 169.6 all-reduce.4
where the time goes:
time: 425 us; the launch traced here: 424 us
  waiting for transfers between devices  164 us (39%)
  matrix products  90.2 us (21%)
  local copies, waits for them, and re-layouts  66.3 us (16%)
  blocking collectives  30.7 us (7%)
  other arithmetic  28.2 us (7%)
  starting transfers between devices  24.6 us (6%)
  between operations  16.8 us (4%)
    psum x1, waiting for transfers between devices, per_device(): summed = lax.psum(local_terms, ('dp', 'ctx'))  135 us
    unnamed x31, local copies, waits for them, and re-layouts  41.6 us
    psum x1, blocking collectives, per_device(): divergence_total = lax.psum(divergence_q + divergence_k, 'ctx')  30.7 us
    dot_general x4, matrix products, relation_advance(): jnp.einsum('hrk,khd->rhd', weights, student_block, preferred_element_type...  28.9 us
    ppermute x8, waiting for transfers between devices, shifted(): lax.ppermute(value, axis, [(source, source + steps) for source in range(f...  28.6 us
    ppermute x8, starting transfers between devices, shifted(): lax.ppermute(value, axis, [(source, source + steps) for source in range(f...  24.6 us
    reduce_sum x4, other arithmetic, online_update(): jnp.sum(jnp.where(allowed, jnp.exp(scores - new_high[:, :, None]), 0.0),...  20.9 us
    dot_general x4, matrix products, relation_advance(): jnp.einsum('rhd,khd->hrk', teacher_here, teacher_block, preferred_element...  17 us
  transfers between devices with their start and end apart: 9, of which 3 were waited for; matrix products, arithmetic and copies ran while one was open for 5% of the time, Pallas kernels for 0%

commit v1 on v0

v1 whole, which is shorter than its diff:
```python
import math

import jax
import jax.numpy as jnp
from jax import lax
from jax.experimental import pallas as pl
from jax.experimental.pallas import tpu as pltpu
from jax.sharding import PartitionSpec as P

H = 16
TDH = 128
SDH = 48
DOCS = 8
ROWS = 128
SLOTS = 256
TAIL = 64
DS = 1536
TW = H * TDH
SW = H * SDH
LOSS_SCALE = 1048576.0
MASKED = -1e30
LOG2E = math.log2(math.e)
BF = jnp.bfloat16
F32 = jnp.float32
MESH = pl.DeviceIdType.MESH

PARTS = 3
ORDERS = (("y", "z", "x"), ("x", "y", "z"), ("z", "x", "y"))
EXTENT = {"xl": 2, "z": 4, "y": 4, "xh": 2}
UNIT = (48, 128)


def dims_of(axis):
    return ("xl", "xh") if axis == "x" else (axis,)


def stage_dims(order):
    dims = ("xl", "z", "y", "xh")
    found = [dims]
    for axis in order:
        dims = tuple(d for d in dims if d not in dims_of(axis))
        found.append(dims)
    return found


def extent(dims):
    return tuple(EXTENT[d] for d in dims)


def kernel(
    tq,
    tk,
    hid,
    wq,
    wk,
    lengths,
    out_loss,
    out_hidden,
    out_wq,
    out_wk,
    T,
    Ttail,
    Hd,
    Htail,
    HdT,
    Wown,
    Woth,
    S,
    E,
    G,
    Gb,
    GX,
    GT,
    Wb,
    agbuf,
    lossb,
    lossr,
    *rest,
):
    sums = rest[: 3 * PARTS + PARTS]
    recvs = rest[4 * PARTS : 4 * PARTS + 3 * PARTS]
    loc, tail_s, tail_r, rs_s, rs_r, ag_s, ag_r, loss_s, loss_r = rest[7 * PARTS :]

    dp = lax.axis_index("dp")
    ctx = lax.axis_index("ctx")
    y, xh = lax.div(dp, 2), lax.rem(dp, 2)
    core = lax.rem(ctx, 2)
    k = lax.div(ctx, 2)
    z, xl = lax.rem(k, 4), lax.div(k, 4)
    x = xh * 2 + xl
    coords = {"x": x, "y": y, "z": z}

    def device(x_, y_, z_, core_):
        return {"dp": y_ * 2 + lax.div(x_, 2), "ctx": (lax.rem(x_, 2) * 4 + z_) * 2 + core_}

    def along(axis, j):
        c = dict(coords)
        c[axis] = lax.rem(c[axis] + j, 4)
        return device(c["x"], c["y"], c["z"], core), c[axis]

    pair = {"dp": dp, "ctx": k * 2 + 1 - core}
    is0, is1 = core == 0, core == 1
    has_next, has_prev = k < 7, k > 0
    sends = jnp.logical_and(is1, has_next)

    mine = pl.ds(pl.multiple_of(core * ROWS, ROWS), ROWS)
    theirs = pl.ds(pl.multiple_of((1 - core) * ROWS, ROWS), ROWS)
    own_hidden = pltpu.make_async_copy(hid, Hd.at[mine], loc.at[0])
    own_hidden.start()

    def by_core(first, second, dst, sem):
        def go(src):
            def start():
                pltpu.make_async_copy(src, dst, sem).start()

            return start

        pl.when(is0)(go(first))
        pl.when(is1)(go(second))
        return pltpu.make_async_copy(first, dst, sem)

    w_own = by_core(wq, wk, Wown, loc.at[1])
    own_t = by_core(tq, tk, T.at[mine], loc.at[2])
    w_oth = by_core(wk, wq, Woth, loc.at[3])

    barrier = pltpu.get_barrier_semaphore()

    def hail(device_id):
        pl.semaphore_signal(barrier, inc=1, device_id=device_id, device_id_type=MESH)

    hail(pair)
    for j in range(1, 8):
        for c in range(2):
            hail({"dp": lax.rem(dp + j, 8), "ctx": k * 2 + c})
    for axis, j in (("x", 1), ("x", 3), ("z", 1), ("z", 2), ("z", 3)):
        hail(along(axis, j)[0])

    @pl.when(sends)
    def _():
        hail({"dp": dp, "ctx": k * 2 + 2})
        hail({"dp": dp, "ctx": k * 2 + 3})

    @pl.when(has_prev)
    def _():
        hail({"dp": dp, "ctx": k * 2 - 1})

    pl.semaphore_wait(
        barrier, 20 + jnp.where(sends, 2, 0) + jnp.where(has_prev, 1, 0)
    )

    pending = []

    def remote(src, dst, send_sem, recv_sem, device_id, cond=None):
        copy = pltpu.make_async_remote_copy(
            src_ref=src,
            dst_ref=dst,
            send_sem=send_sem,
            recv_sem=recv_sem,
            device_id=device_id,
            device_id_type=MESH,
        )
        if cond is None:
            copy.start()
        else:
            pl.when(cond)(copy.start)
        pending.append((copy, cond))
        return copy

    def arrived(dst, recv_sem, cond=None):
        copy = pltpu.make_async_remote_copy(
            src_ref=dst,
            dst_ref=dst,
            send_sem=recv_sem,
            recv_sem=recv_sem,
            device_id=pair,
            device_id_type=MESH,
        )
        if cond is None:
            copy.wait_recv()
        else:
            pl.when(cond)(copy.wait_recv)

    last = pl.ds(ROWS - TAIL, TAIL)
    remote(hid, Hd.at[mine], tail_s.at[0], tail_r.at[0], pair)
    for c in range(2):
        remote(
            hid.at[last], Htail, tail_s.at[1 + c], tail_r.at[1], {"dp": dp, "ctx": k * 2 + 2 + c}, sends
        )
    remote(tk, T.at[mine], tail_s.at[3], tail_r.at[2], pair, is0)
    remote(tq, T.at[mine], tail_s.at[3], tail_r.at[2], pair, is1)
    chunk = 512
    for q in range(TW // chunk):
        cols = pl.ds(q * chunk, chunk)
        for c, src in enumerate((tq, tk)):
            remote(
                src.at[last, cols],
                Ttail.at[:, cols],
                tail_s.at[4 + 2 * q + c],
                tail_r.at[3 + q],
                {"dp": dp, "ctx": k * 2 + 2 + c},
                sends,
            )

    start = jnp.int32(0)
    end = jnp.int32(0)
    count = jnp.int32(0)
    for i in range(DOCS):
        value = lengths[0, i]
        start = start + jnp.where(i < k, value, 0)
        end = end + jnp.where(i <= k, value, 0)
        count = count + value
    lo = end - SLOTS * k
    hi = start - SLOTS * (k - 1)
    mean_over = 1.0 / (H * jnp.full((1, 128), count, jnp.int32).astype(F32))
    coefficient = LOSS_SCALE * mean_over

    def slot(shape, first):
        return lax.broadcasted_iota(jnp.int32, shape, 0) + first

    def tail_mask(width):
        return slot((TAIL, width), SLOTS - TAIL) >= hi

    own_hidden.wait()
    w_own.wait()
    arrived(Hd.at[theirs], tail_r.at[0])
    for r in range(0, SLOTS, 128):
        S[r : r + 128, :] = jnp.dot(
            Hd[r : r + 128, :], Wown[...], preferred_element_type=F32
        ).astype(BF)
    arrived(Htail, tail_r.at[1], has_prev)
    tail_rows = slice(SLOTS - TAIL, SLOTS)
    projected = jnp.dot(Htail[...], Wown[...], preferred_element_type=F32).astype(BF)
    S[tail_rows, :] = jnp.where(tail_mask(SW), projected, S[tail_rows, :])
    Hd[tail_rows, :] = jnp.where(tail_mask(DS), Htail[...], Hd[tail_rows, :])
    for r in range(0, DS, 128):
        HdT[r : r + 128, :] = Hd[:, r : r + 128].T

    own_t.wait()
    arrived(T.at[theirs], tail_r.at[2])

    row_slot = lax.broadcasted_iota(jnp.int32, (SLOTS, 128), 0)
    row_lane = lax.broadcasted_iota(jnp.int32, (SLOTS, 128), 1)
    row_bad = jnp.logical_and(row_slot >= lo, row_slot < hi)
    row_bias = jnp.where(row_bad, MASKED, 0.0)
    bias_tile = jnp.where(row_lane == 0, row_bias, 0.0).astype(BF)
    one_tile = jnp.where(row_lane == 0, 1.0, 0.0).astype(BF)
    bias_all = row_bias.astype(BF)
    rate = []
    for cb in range(2):
        lane_slot = lax.broadcasted_iota(jnp.int32, (1, 128), 1) + 128 * cb
        good = jnp.logical_or(lane_slot < lo, lane_slot >= hi)
        rate.append(jnp.where(good, coefficient, 0.0))
    ct = LOG2E / math.sqrt(TDH)
    cs = LOG2E / math.sqrt(SDH)
    nt = (((1,), (1,)), ((), ()))

    G[...] = jnp.zeros_like(G)

    def probabilities(scores, factor, rate_here):
        high = jnp.max(scores, axis=0, keepdims=True)
        rel = (scores - high) * factor
        raw = jnp.exp2(rel)
        total = jnp.sum(raw, axis=0, keepdims=True)
        return rel, raw * (rate_here / total), jnp.log2(total)

    def head(h, loss):
        th = T[:, TDH * h : TDH * (h + 1)]
        lhs_t = jnp.concatenate([th, bias_tile], axis=1)
        rhs_t = jnp.concatenate([th, one_tile], axis=1)
        first = SDH * h
        a, b = first // 128, (first + SDH - 1) // 128
        width = (b - a + 1) * 128
        cols = slice(128 * a, 128 * a + width)
        st = S[:, cols]
        lane = lax.broadcasted_iota(jnp.int32, (SLOTS, width), 1) + 128 * a
        inside = jnp.logical_and(lane >= first, lane < first + SDH)
        spare = 128 * a if first > 128 * a else 128 * a + width - 1
        picked = jnp.where(inside, st, jnp.zeros_like(st))
        wide_bias = bias_all if width == 128 else jnp.concatenate([bias_all, bias_all], axis=1)
        lhs_s = jnp.where(lane == spare, wide_bias, picked)
        rhs_s = jnp.where(lane == spare, jnp.ones_like(st), st)
        for cb in range(2):
            block = slice(128 * cb, 128 * (cb + 1))
            t = lax.dot_general(lhs_t, rhs_t[block], nt, preferred_element_type=F32)
            s = lax.dot_general(lhs_s, rhs_s[block], nt, preferred_element_type=F32)
            rel_t, et, log_t = probabilities(t, ct, rate[cb])
            rel_s, es, log_s = probabilities(s, cs, rate[cb])
            E[:, block] = es - et
            loss = loss + jnp.sum(et * (rel_t - rel_s), axis=0, keepdims=True)
            loss = loss - rate[cb] * (log_t - log_s)
        e00, e01 = E[:128, :128], E[:128, 128:]
        e10, e11 = E[128:, :128], E[128:, 128:]
        w01 = e01 + e10.T
        Wb[:128, :128] = (e00 + e00.T).astype(BF)
        Wb[:128, 128:] = w01.astype(BF)
        Wb[128:, :128] = w01.T.astype(BF)
        Wb[128:, 128:] = (e11 + e11.T).astype(BF)
        G[:, cols] += jnp.dot(Wb[...], picked, preferred_element_type=F32)
        return loss

    def sub(ref, dims, axis, at):
        index = []
        for d in dims:
            if d not in dims_of(axis):
                index.append(slice(None))
            elif d == "xl":
                index.append(lax.rem(at, 2))
            elif d == "xh":
                index.append(lax.div(at, 2))
            else:
                index.append(at)
        return ref.at[tuple(index)]

    def send_stage(p, stage):
        order = ORDERS[p]
        dims = stage_dims(order)[stage]
        source = sums[4 * p + stage]
        for j in (2, 1, 3):
            peer, at = along(order[stage], j)
            n = (p * 3 + stage) * 3 + j - 1
            remote(
                sub(source, dims, order[stage], at),
                recvs[3 * p + stage].at[j - 1],
                rs_s.at[n],
                rs_r.at[n],
                peer,
            )

    def sum_stage(p, stage):
        order = ORDERS[p]
        dims = stage_dims(order)[stage]
        buf = recvs[3 * p + stage]
        total = sub(sums[4 * p + stage], dims, order[stage], coords[order[stage]])[...].astype(F32)
        for j in (1, 3, 2):
            arrived(buf.at[j - 1], rs_r.at[(p * 3 + stage) * 3 + j - 1])
            total = total + buf[j - 1].astype(F32)
        sums[4 * p + stage + 1][...] = total.astype(BF)

    def part_terms(p):
        cols = slice(256 * p, 256 * (p + 1))
        Gb[:, cols] = (G[:, cols] * (1.0 / math.sqrt(SDH))).astype(BF)
        for xl_ in range(2):
            terms = jnp.dot(
                HdT[768 * xl_ : 768 * (xl_ + 1), :], Gb[:, cols], preferred_element_type=F32
            ).astype(BF)
            for xh_ in range(2):
                sums[4 * p][xl_, :, :, xh_] = terms[:, 128 * xh_ : 128 * (xh_ + 1)].reshape(
                    (4, 4) + UNIT
                )
        send_stage(p, 0)

    yl = lax.rem(y, 2)
    goal = lax.div(y, 2)

    def send_final(p):
        block = sums[4 * p + 3]
        for j in range(8):
            dp_ = lax.rem(dp + j, 8)
            n = p * 8 + j
            cond = None if j else core != goal
            remote(
                block,
                agbuf.at[core, p, yl, xh],
                ag_s.at[n],
                ag_r.at[core, p, yl, xh],
                {"dp": dp_, "ctx": k * 2 + goal},
                cond,
            )

        @pl.when(core == goal)
        def _():
            agbuf[core, p, yl, xh] = block[...]

    loss = jnp.zeros((1, 128), F32)
    for h in range(H):
        if h % 4 == 0:
            cols = slice(TDH * h, TDH * (h + 4))
            arrived(Ttail.at[:, cols], tail_r.at[3 + h // 4], has_prev)
            T[tail_rows, cols] = jnp.where(tail_mask(TDH * 4), Ttail[:, cols], T[tail_rows, cols])
        loss = head(h, loss)
        if h == 5:
            part_terms(0)
        if h == 10:
            part_terms(1)
        if h == 15:
            part_terms(2)

    remote(Gb.at[theirs], GX, tail_s.at[12], tail_r.at[7], pair)
    remote(
        Gb.at[tail_rows],
        GT.at[core],
        tail_s.at[13],
        tail_r.at[8 + core],
        {"dp": dp, "ctx": k * 2 - 1},
        has_prev,
    )
    lossb[0] = jnp.broadcast_to(loss, (8, 128))
    for j in (1, 2, 3):
        remote(lossb.at[0], lossr.at[j - 1], loss_s.at[j - 1], loss_r.at[j - 1], along("z", j)[0])

    sum_stage(0, 0)
    send_stage(0, 1)
    sum_stage(1, 0)
    send_stage(1, 1)

    w_oth.wait()
    arrived(GX, tail_r.at[7])
    for c in range(2):
        arrived(GT.at[c], tail_r.at[8 + c], sends)
    rows = slice(ROWS - TAIL, ROWS)
    lent = slot((TAIL, SW), SLOTS - TAIL - ROWS + core * ROWS) >= lo
    zero = jnp.zeros((TAIL, SW), BF)
    keep = jnp.full((TAIL, SW), k, jnp.int32) < 7
    own_low = Gb[pl.ds(pl.multiple_of(core * ROWS, ROWS), ROWS - TAIL), :]
    own_high = Gb[pl.ds(pl.multiple_of(core * ROWS + ROWS - TAIL, TAIL), TAIL), :]
    own_high = jnp.where(lent, jnp.where(keep, GT[1], zero), own_high)
    GX[rows, :] = jnp.where(lent, jnp.where(keep, GT[0], zero), GX[rows, :])
    own_rows = jnp.concatenate([own_low, own_high], axis=0)
    for r in range(0, DS, 512):
        out_hidden[:, r : r + 512] = (
            lax.dot_general(own_rows, Wown[r : r + 512, :], nt, preferred_element_type=F32)
            + lax.dot_general(GX[...], Woth[r : r + 512, :], nt, preferred_element_type=F32)
        ).astype(BF)

    sum_stage(2, 0)
    send_stage(2, 1)
    for p in range(PARTS):
        sum_stage(p, 1)
        send_stage(p, 2)

    loss_total = lossb[0]
    for j in (1, 2, 3):
        arrived(lossr.at[j - 1], loss_r.at[j - 1])
        loss_total = loss_total + lossr[j - 1]
    lossb[1] = loss_total
    x_other = xh * 2 + 1 - xl
    remote(lossb.at[1], lossr.at[3], loss_s.at[3], loss_r.at[3], device(x_other, y, z, core))

    for p in range(PARTS):
        sum_stage(p, 2)
        send_final(p)

    arrived(lossr.at[3], loss_r.at[3])
    loss_total = loss_total + lossr[3]
    lossb[2] = loss_total
    remote(lossb.at[2], lossr.at[4], loss_s.at[4], loss_r.at[4], pair)
    arrived(lossr.at[4], loss_r.at[4])
    loss_total = loss_total + lossr[4]
    out_loss[...] = jnp.broadcast_to(
        jnp.sum(loss_total[:1], axis=1, keepdims=True) * (math.log(2.0) / LOSS_SCALE), (1, 128)
    )

    for p in range(PARTS):
        for r, out in enumerate((out_wq, out_wk)):
            for yl_ in range(2):
                for xh_ in range(2):
                    itself = jnp.logical_and(
                        jnp.logical_and(core == r, xh == xh_), y == 2 * core + yl_
                    )
                    arrived(
                        agbuf.at[r, p, yl_, xh_],
                        ag_r.at[r, p, yl_, xh_],
                        jnp.logical_not(itself),
                    )
                    at = 256 * p + 128 * xh_
                    out[48 * yl_ : 48 * (yl_ + 1), at : at + 128] = agbuf[r, p, yl_, xh_].astype(F32)

    for copy, cond in pending:
        if cond is None:
            copy.wait_send()
        else:
            pl.when(cond)(copy.wait_send)


def per_device(teacher_query, teacher_key, student_hidden, weight_query, weight_key, doc_lengths):
    scratch = [
        pltpu.VMEM((SLOTS, TW), BF),
        pltpu.VMEM((TAIL, TW), BF),
        pltpu.VMEM((SLOTS, DS), BF),
        pltpu.VMEM((TAIL, DS), BF),
        pltpu.VMEM((DS, SLOTS), BF),
        pltpu.VMEM((DS, SW), BF),
        pltpu.VMEM((DS, SW), BF),
        pltpu.VMEM((SLOTS, SW), BF),
        pltpu.VMEM((SLOTS, SLOTS), F32),
        pltpu.VMEM((SLOTS, SW), F32),
        pltpu.VMEM((SLOTS, SW), BF),
        pltpu.VMEM((ROWS, SW), BF),
        pltpu.VMEM((2, TAIL, SW), BF),
        pltpu.VMEM((SLOTS, SLOTS), BF),
        pltpu.VMEM((2, PARTS, 2, 2) + UNIT, BF),
        pltpu.VMEM((3, 8, 128), F32),
        pltpu.VMEM((5, 8, 128), F32),
    ]
    for order in ORDERS:
        for dims in stage_dims(order):
            scratch.append(pltpu.VMEM(extent(dims) + UNIT, BF))
    for order in ORDERS:
        for dims in stage_dims(order)[1:]:
            scratch.append(pltpu.VMEM((3,) + extent(dims) + UNIT, BF))
    dma = pltpu.SemaphoreType.DMA
    scratch += [
        dma((4,)),
        dma((14,)),
        dma((10,)),
        dma((27,)),
        dma((27,)),
        dma((24,)),
        dma((2, PARTS, 2, 2)),
        dma((5,)),
        dma((5,)),
    ]
    vmem = pl.BlockSpec(memory_space=pltpu.VMEM)
    anywhere = pl.BlockSpec(memory_space=pl.ANY)
    loss, hidden_grad, grad_wq, grad_wk = pl.pallas_call(
        kernel,
        out_shape=(
            jax.ShapeDtypeStruct((1, 128), F32),
            jax.ShapeDtypeStruct((ROWS, DS), BF),
            jax.ShapeDtypeStruct((96, SW), F32),
            jax.ShapeDtypeStruct((96, SW), F32),
        ),
        in_specs=[anywhere] * 5 + [pl.BlockSpec(memory_space=pltpu.SMEM)],
        out_specs=(vmem, vmem, vmem, vmem),
        scratch_shapes=scratch,
        compiler_params=pltpu.CompilerParams(
            collective_id=0, has_side_effects=True, vmem_limit_bytes=56 * 1024 * 1024
        ),
        name="relations",
    )(
        teacher_query[0],
        teacher_key[0],
        student_hidden[0],
        weight_query,
        weight_key,
        doc_lengths,
    )
    return loss[0, :1], hidden_grad[None], grad_wq, grad_wk


def solution(mesh):
    in_specs = (
        P("dp", "ctx", None),
        P("dp", "ctx", None),
        P("dp", "ctx", None),
        P(),
        P(),
        P("dp", None),
    )
    out_specs = (P("dp"), P("dp", "ctx", None), P("ctx", None), P("ctx", None))
    return jax.shard_map(
        per_device, mesh=mesh, in_specs=in_specs, out_specs=out_specs, check_vma=False
    )
```

time: 425 us -> 60.3 us (0.14)
  waiting for transfers between devices: 164 us -> 0 us
  matrix products: 90.2 us -> 0 us
  local copies, waits for them, and re-layouts: 66.3 us -> 5.15 us
  Pallas kernels: 0 us -> 52.6 us
  blocking collectives: 30.7 us -> 0 us
  other arithmetic: 28.2 us -> 0 us
  starting transfers between devices: 24.6 us -> 0 us
  between operations: 16.8 us -> 2.32 us
    psum x1 -> x0, waiting for transfers between devices: 135 us -> none  [per_device(): summed = lax.psum(local_terms, ('dp', 'ctx'))]
    dot_general x25 -> x0, matrix products: 90.2 us -> none  [the longest x4 28.9 us: relation_advance(): jnp.einsum('hrk,khd->rhd', weights, student_block, preferred_element_type...]
    pallas_call x0 -> x1, Pallas kernels: none -> 52.6 us  [per_device(): pl.pallas_call(kernel, out_shape=(jax.ShapeDtypeStruct((1, 128), F32), ja...]
    unnamed x31 -> x3, local copies, waits for them, and re-layouts: 41.6 us -> 5.15 us
    psum x1 -> x0, blocking collectives: 30.7 us -> none  [per_device(): divergence_total = lax.psum(divergence_q + divergence_k, 'ctx')]
    ppermute x8 -> x0, waiting for transfers between devices: 28.6 us -> none  [shifted(): lax.ppermute(value, axis, [(source, source + steps) for source in range(f...]
    ppermute x8 -> x0, starting transfers between devices: 24.6 us -> none  [shifted(): lax.ppermute(value, axis, [(source, source + steps) for source in range(f...]
    reduce_sum x7 -> x0, other arithmetic: 21.7 us -> none  [the longest x4 20.9 us: online_update(): jnp.sum(jnp.where(allowed, jnp.exp(scores - new_high[:, :, None]), 0.0),...]
  transfers between devices with their start and end apart: 9 -> 0, of which waited for: 3 -> 0; matrix products, arithmetic and copies ran while one was open for 5% -> 0% of each run, Pallas kernels for 0% -> 0%
where the time goes in v1:
time: 60.3 us; the launch traced here: 60 us
  Pallas kernels  52.6 us (87%)
  local copies, waits for them, and re-layouts  5.15 us (9%)
  between operations  2.32 us (4%)
    pallas_call x1, Pallas kernels, per_device(): pl.pallas_call(kernel, out_shape=(jax.ShapeDtypeStruct((1, 128), F32), ja...  52.6 us
    unnamed x3, local copies, waits for them, and re-layouts  5.15 us

profile of v1, /device:TPU:1, one launch (start us, length us, event | category | flops | bytes accessed | tf_op | source)
XLA Modules:
  0.0 60.0 jit_solution(18304757916036258915)
XLA Ops:
  0.6 52.6 %relations.1 = (f32[1,128]{1,0:T(1,128)}, bf16[128,1536]{1,0:T(8,128)(2,1)}, f32[96,768]{1,0:T(8,128)}, f32[96,768]{1,0:T(8,128)}) custom-call(bf16[128,2048]{1,0:T(8,128)(2,1)} %bitcast.6, bf16[128,2048]{1,0:T(8,128)(2,1)} %bitcast.7, bf16[128,1536]{1,0:T(8,128)(2,1)} %bitcast.8, bf16[1536,768]{1,0:T(8,128)(2,1)} %wq.1, bf16[1536,768]{1,0:T(8,128)(2,1)} %wk.1, ...), custom_call_target="tpu_custom_call" | custom-call | tf_op jit(solution)/shard_map/relations/pallas_call | solution.py:515
  53.8 1.8 %copy.15 = bf16[1,128,1536]{2,1,0:T(8,128)(2,1)} copy(bf16[1,128,1536]{2,1,0:T(8,128)(2,1)} %bitcast.9) | data formatting | bytes 786432
  55.5 1.7 %copy.16 = f32[96,768]{1,0:T(8,128)} copy(f32[96,768]{1,0:T(8,128)} %get-tuple-element.18) | data formatting | bytes 589824
  57.2 1.7 %copy.17 = f32[96,768]{1,0:T(8,128)} copy(f32[96,768]{1,0:T(8,128)} %get-tuple-element.19) | data formatting | bytes 589824

commit v2 on v1

--- a/solution.py
+++ b/solution.py
@@ -24,10 +24,14 @@
 F32 = jnp.float32
 MESH = pl.DeviceIdType.MESH
 
+CHUNKS = 3
 PARTS = 3
-ORDERS = (("y", "z", "x"), ("x", "y", "z"), ("z", "x", "y"))
+XYZ, YZX, ZXY = ("x", "y", "z"), ("y", "z", "x"), ("z", "x", "y")
+ORDERS = ((XYZ, YZX, XYZ), (YZX, XYZ, YZX), (ZXY, ZXY, XYZ))
+READY = (5, 10, 15)
 EXTENT = {"xl": 2, "z": 4, "y": 4, "xh": 2}
-UNIT = (48, 128)
+UNIT = (16, 128)
+GROUPS_OF_HEADS = ((0, 4), (4, 8), (8, 12), (12, 14), (14, 16))
 
 
 def dims_of(axis):
@@ -56,8 +60,7 @@
     lengths,
     out_loss,
     out_hidden,
-    out_wq,
-    out_wk,
+    out_terms,
     T,
     Ttail,
     Hd,
@@ -77,9 +80,10 @@
     lossr,
     *rest,
 ):
-    sums = rest[: 3 * PARTS + PARTS]
-    recvs = rest[4 * PARTS : 4 * PARTS + 3 * PARTS]
-    loc, tail_s, tail_r, rs_s, rs_r, ag_s, ag_r, loss_s, loss_r = rest[7 * PARTS :]
+    pieces = CHUNKS * PARTS
+    sums = rest[: 3 * pieces]
+    recvs = rest[3 * pieces : 6 * pieces]
+    final, loc, tail_s, tail_r, rs_s, rs_r, ag_s, ag_r, loss_s, loss_r = rest[6 * pieces :]
 
     dp = lax.axis_index("dp")
     ctx = lax.axis_index("ctx")
@@ -181,16 +185,22 @@
             pl.when(cond)(copy.wait_recv)
 
     last = pl.ds(ROWS - TAIL, TAIL)
+    half = DS // 2
     remote(hid, Hd.at[mine], tail_s.at[0], tail_r.at[0], pair)
     for c in range(2):
+        cols = pl.ds(c * half, half)
         remote(
-            hid.at[last], Htail, tail_s.at[1 + c], tail_r.at[1], {"dp": dp, "ctx": k * 2 + 2 + c}, sends
+            hid.at[last, cols],
+            Htail.at[:, cols],
+            tail_s.at[1 + c],
+            tail_r.at[1],
+            {"dp": dp, "ctx": k * 2 + 2 + c},
+            sends,
         )
     remote(tk, T.at[mine], tail_s.at[3], tail_r.at[2], pair, is0)
     remote(tq, T.at[mine], tail_s.at[3], tail_r.at[2], pair, is1)
-    chunk = 512
-    for q in range(TW // chunk):
-        cols = pl.ds(q * chunk, chunk)
+    for q, (h0, h1) in enumerate(GROUPS_OF_HEADS):
+        cols = pl.ds(TDH * h0, TDH * (h1 - h0))
         for c, src in enumerate((tq, tk)):
             remote(
                 src.at[last, cols],
@@ -227,7 +237,10 @@
         S[r : r + 128, :] = jnp.dot(
             Hd[r : r + 128, :], Wown[...], preferred_element_type=F32
         ).astype(BF)
-    arrived(Htail, tail_r.at[1], has_prev)
+    my_half = Htail.at[:, pl.ds(pl.multiple_of(core * half, half), half)]
+    arrived(my_half, tail_r.at[1], has_prev)
+    remote(my_half, my_half, tail_s.at[14], tail_r.at[11], pair, has_prev)
+    arrived(my_half, tail_r.at[11], has_prev)
     tail_rows = slice(SLOTS - TAIL, SLOTS)
     projected = jnp.dot(Htail[...], Wown[...], preferred_element_type=F32).astype(BF)
     S[tail_rows, :] = jnp.where(tail_mask(SW), projected, S[tail_rows, :])
@@ -311,86 +324,97 @@
                 index.append(at)
         return ref.at[tuple(index)]
 
-    def send_stage(p, stage):
-        order = ORDERS[p]
+    def send_stage(c, p, stage):
+        order = ORDERS[c][p]
         dims = stage_dims(order)[stage]
-        source = sums[4 * p + stage]
+        piece = c * PARTS + p
+        source = sums[3 * piece + stage]
         for j in (2, 1, 3):
             peer, at = along(order[stage], j)
-            n = (p * 3 + stage) * 3 + j - 1
+            n = (piece * 3 + stage) * 3 + j - 1
             remote(
                 sub(source, dims, order[stage], at),
-                recvs[3 * p + stage].at[j - 1],
+                recvs[3 * piece + stage].at[j - 1],
                 rs_s.at[n],
                 rs_r.at[n],
                 peer,
             )
 
-    def sum_stage(p, stage):
-        order = ORDERS[p]
+    def sum_stage(c, p, stage):
+        order = ORDERS[c][p]
         dims = stage_dims(order)[stage]
-        buf = recvs[3 * p + stage]
-        total = sub(sums[4 * p + stage], dims, order[stage], coords[order[stage]])[...].astype(F32)
+        piece = c * PARTS + p
+        buf = recvs[3 * piece + stage]
+        total = sub(sums[3 * piece + stage], dims, order[stage], coords[order[stage]])[...].astype(F32)
         for j in (1, 3, 2):
-            arrived(buf.at[j - 1], rs_r.at[(p * 3 + stage) * 3 + j - 1])
+            arrived(buf.at[j - 1], rs_r.at[(piece * 3 + stage) * 3 + j - 1])
             total = total + buf[j - 1].astype(F32)
-        sums[4 * p + stage + 1][...] = total.astype(BF)
-
-    def part_terms(p):
-        cols = slice(256 * p, 256 * (p + 1))
+        if stage < 2:
+            sums[3 * piece + stage + 1][...] = total.astype(BF)
+        else:
+            final[c, 16 * p : 16 * (p + 1)] = total.astype(BF)
+
+    def advance(c, stage):
+        for p in range(PARTS):
+            sum_stage(c, p, stage)
+            if stage < 2:
+                send_stage(c, p, stage + 1)
+        if stage == 2:
+            send_final(c)
+
+    def chunk_terms(c):
+        cols = slice(256 * c, 256 * (c + 1))
         Gb[:, cols] = (G[:, cols] * (1.0 / math.sqrt(SDH))).astype(BF)
         for xl_ in range(2):
-            terms = jnp.dot(
-                HdT[768 * xl_ : 768 * (xl_ + 1), :], Gb[:, cols], preferred_element_type=F32
-            ).astype(BF)
-            for xh_ in range(2):
-                sums[4 * p][xl_, :, :, xh_] = terms[:, 128 * xh_ : 128 * (xh_ + 1)].reshape(
-                    (4, 4) + UNIT
-                )
-        send_stage(p, 0)
+            terms = (
+                jnp.dot(HdT[768 * xl_ : 768 * (xl_ + 1), :], Gb[:, cols], preferred_element_type=F32)
+                .astype(BF)
+                .reshape(4, 4, PARTS, 16, 256)
+            )
+            for p in range(PARTS):
+                for xh_ in range(2):
+                    sums[3 * (c * PARTS + p)][xl_, :, :, xh_] = terms[
+                        :, :, p, :, 128 * xh_ : 128 * (xh_ + 1)
+                    ]
+        for p in range(PARTS):
+            send_stage(c, p, 0)
 
     yl = lax.rem(y, 2)
     goal = lax.div(y, 2)
 
-    def send_final(p):
-        block = sums[4 * p + 3]
+    def send_final(c):
         for j in range(8):
-            dp_ = lax.rem(dp + j, 8)
-            n = p * 8 + j
-            cond = None if j else core != goal
             remote(
-                block,
-                agbuf.at[core, p, yl, xh],
-                ag_s.at[n],
-                ag_r.at[core, p, yl, xh],
-                {"dp": dp_, "ctx": k * 2 + goal},
-                cond,
+                final.at[c],
+                agbuf.at[core, c, yl, xh],
+                ag_s.at[c * 8 + j],
+                ag_r.at[core, c, yl, xh],
+                {"dp": lax.rem(dp + j, 8), "ctx": k * 2 + goal},
+                None if j else core != goal,
             )
 
         @pl.when(core == goal)
         def _():
-            agbuf[core, p, yl, xh] = block[...]
+            agbuf[core, c, yl, xh] = final[c]
 
     loss = jnp.zeros((1, 128), F32)
-    for h in range(H):
-        if h % 4 == 0:
-            cols = slice(TDH * h, TDH * (h + 4))
-            arrived(Ttail.at[:, cols], tail_r.at[3 + h // 4], has_prev)
-            T[tail_rows, cols] = jnp.where(tail_mask(TDH * 4), Ttail[:, cols], T[tail_rows, cols])
-        loss = head(h, loss)
-        if h == 5:
-            part_terms(0)
-        if h == 10:
-            part_terms(1)
-        if h == 15:
-            part_terms(2)
-
-    remote(Gb.at[theirs], GX, tail_s.at[12], tail_r.at[7], pair)
+    for q, (h0, h1) in enumerate(GROUPS_OF_HEADS):
+        cols = slice(TDH * h0, TDH * h1)
+        arrived(Ttail.at[:, cols], tail_r.at[3 + q], has_prev)
+        T[tail_rows, cols] = jnp.where(
+            tail_mask(TDH * (h1 - h0)), Ttail[:, cols], T[tail_rows, cols]
+        )
+        for h in range(h0, h1):
+            loss = head(h, loss)
+            if h in READY:
+                chunk_terms(READY.index(h))
+
+    remote(Gb.at[theirs], GX, tail_s.at[15], tail_r.at[8], pair)
     remote(
         Gb.at[tail_rows],
         GT.at[core],
-        tail_s.at[13],
-        tail_r.at[8 + core],
+        tail_s.at[16],
+        tail_r.at[9 + core],
         {"dp": dp, "ctx": k * 2 - 1},
         has_prev,
     )
@@ -398,15 +422,12 @@
     for j in (1, 2, 3):
         remote(lossb.at[0], lossr.at[j - 1], loss_s.at[j - 1], loss_r.at[j - 1], along("z", j)[0])
 
-    sum_stage(0, 0)
-    send_stage(0, 1)
-    sum_stage(1, 0)
-    send_stage(1, 1)
+    advance(0, 0)
 
     w_oth.wait()
-    arrived(GX, tail_r.at[7])
+    arrived(GX, tail_r.at[8])
     for c in range(2):
-        arrived(GT.at[c], tail_r.at[8 + c], sends)
+        arrived(GT.at[c], tail_r.at[9 + c], sends)
     rows = slice(ROWS - TAIL, ROWS)
     lent = slot((TAIL, SW), SLOTS - TAIL - ROWS + core * ROWS) >= lo
     zero = jnp.zeros((TAIL, SW), BF)
@@ -422,11 +443,11 @@
             + lax.dot_general(GX[...], Woth[r : r + 512, :], nt, preferred_element_type=F32)
         ).astype(BF)
 
-    sum_stage(2, 0)
-    send_stage(2, 1)
-    for p in range(PARTS):
-        sum_stage(p, 1)
-        send_stage(p, 2)
+    advance(1, 0)
+    advance(0, 1)
+    advance(2, 0)
+    advance(1, 1)
+    advance(0, 2)
 
     loss_total = lossb[0]
     for j in (1, 2, 3):
@@ -436,9 +457,9 @@
     x_other = xh * 2 + 1 - xl
     remote(lossb.at[1], lossr.at[3], loss_s.at[3], loss_r.at[3], device(x_other, y, z, core))
 
-    for p in range(PARTS):
-        sum_stage(p, 2)
-        send_final(p)
+    advance(2, 1)
+    advance(1, 2)
+    advance(2, 2)
 
     arrived(lossr.at[3], loss_r.at[3])
     loss_total = loss_total + lossr[3]
@@ -450,26 +471,36 @@
         jnp.sum(loss_total[:1], axis=1, keepdims=True) * (math.log(2.0) / LOSS_SCALE), (1, 128)
     )
 
-    for p in range(PARTS):
-        for r, out in enumerate((out_wq, out_wk)):
+    for c in range(CHUNKS):
+        for r in range(2):
             for yl_ in range(2):
                 for xh_ in range(2):
                     itself = jnp.logical_and(
                         jnp.logical_and(core == r, xh == xh_), y == 2 * core + yl_
                     )
                     arrived(
-                        agbuf.at[r, p, yl_, xh_],
-                        ag_r.at[r, p, yl_, xh_],
+                        agbuf.at[r, c, yl_, xh_],
+                        ag_r.at[r, c, yl_, xh_],
                         jnp.logical_not(itself),
                     )
-                    at = 256 * p + 128 * xh_
-                    out[48 * yl_ : 48 * (yl_ + 1), at : at + 128] = agbuf[r, p, yl_, xh_].astype(F32)
+    out_terms[...] = agbuf[...]
 
     for copy, cond in pending:
         if cond is None:
             copy.wait_send()
         else:
             pl.when(cond)(copy.wait_send)
+
+
+def finish(loss, hidden_grad, terms, out_loss, out_hidden, out_wq, out_wk):
+    out_loss[0] = loss[0, 0]
+    out_hidden[...] = hidden_grad[...]
+    for r, out in enumerate((out_wq, out_wk)):
+        for c in range(CHUNKS):
+            for yl in range(2):
+                for xh in range(2):
+                    at = 256 * c + 128 * xh
+                    out[48 * yl : 48 * (yl + 1), at : at + 128] = terms[r, c, yl, xh].astype(F32)
 
 
 def per_device(teacher_query, teacher_key, student_hidden, weight_query, weight_key, doc_lengths):
@@ -488,40 +519,42 @@
         pltpu.VMEM((ROWS, SW), BF),
         pltpu.VMEM((2, TAIL, SW), BF),
         pltpu.VMEM((SLOTS, SLOTS), BF),
-        pltpu.VMEM((2, PARTS, 2, 2) + UNIT, BF),
+        pltpu.VMEM((2, CHUNKS, 2, 2, 48, 128), BF),
         pltpu.VMEM((3, 8, 128), F32),
         pltpu.VMEM((5, 8, 128), F32),
     ]
-    for order in ORDERS:
-        for dims in stage_dims(order):
-            scratch.append(pltpu.VMEM(extent(dims) + UNIT, BF))
-    for order in ORDERS:
-        for dims in stage_dims(order)[1:]:
-            scratch.append(pltpu.VMEM((3,) + extent(dims) + UNIT, BF))
+    for orders in ORDERS:
+        for order in orders:
+            for dims in stage_dims(order)[:3]:
+                scratch.append(pltpu.VMEM(extent(dims) + UNIT, BF))
+    for orders in ORDERS:
+        for order in orders:
+            for dims in stage_dims(order)[1:]:
+                scratch.append(pltpu.VMEM((3,) + extent(dims) + UNIT, BF))
+    scratch.append(pltpu.VMEM((CHUNKS, 48, 128), BF))
     dma = pltpu.SemaphoreType.DMA
     scratch += [
         dma((4,)),
-        dma((14,)),
-        dma((10,)),
-        dma((27,)),
-        dma((27,)),
+        dma((17,)),
+        dma((12,)),
+        dma((81,)),
+        dma((81,)),
         dma((24,)),
-        dma((2, PARTS, 2, 2)),
+        dma((2, CHUNKS, 2, 2)),
         dma((5,)),
         dma((5,)),
     ]
     vmem = pl.BlockSpec(memory_space=pltpu.VMEM)
     anywhere = pl.BlockSpec(memory_space=pl.ANY)
-    loss, hidden_grad, grad_wq, grad_wk = pl.pallas_call(
+    loss, hidden_grad, terms = pl.pallas_call(
         kernel,
         out_shape=(
             jax.ShapeDtypeStruct((1, 128), F32),
             jax.ShapeDtypeStruct((ROWS, DS), BF),
-            jax.ShapeDtypeStruct((96, SW), F32),
-            jax.ShapeDtypeStruct((96, SW), F32),
+            jax.ShapeDtypeStruct((2, CHUNKS, 2, 2, 48, 128), BF),
         ),
         in_specs=[anywhere] * 5 + [pl.BlockSpec(memory_space=pltpu.SMEM)],
-        out_specs=(vmem, vmem, vmem, vmem),
+        out_specs=(vmem, vmem, vmem),
         scratch_shapes=scratch,
         compiler_params=pltpu.CompilerParams(
             collective_id=0, has_side_effects=True, vmem_limit_bytes=56 * 1024 * 1024
@@ -535,7 +568,20 @@
         weight_key,
         doc_lengths,
     )
-    return loss[0, :1], hidden_grad[None], grad_wq, grad_wk
+    smem = pl.BlockSpec(memory_space=pltpu.SMEM)
+    loss, hidden_grad, grad_wq, grad_wk = pl.pallas_call(
+        finish,
+        out_shape=(
+            jax.ShapeDtypeStruct((1,), F32),
+            jax.ShapeDtypeStruct((ROWS, DS), BF),
+            jax.ShapeDtypeStruct((96, SW), F32),
+            jax.ShapeDtypeStruct((96, SW), F32),
+        ),
+        in_specs=[smem, vmem, vmem],
+        out_specs=(smem, vmem, vmem, vmem),
+        name="finish",
+    )(loss, hidden_grad, terms)
+    return loss, hidden_grad[None], grad_wq, grad_wk
 
 
 def solution(mesh):

time: 60.3 us -> 54 us (0.90)
  local copies, waits for them, and re-layouts: 5.15 us -> 0 us
  between operations: 2.32 us -> 0.64 us
    unnamed x3 -> x0, local copies, waits for them, and re-layouts: 5.15 us -> none
    pallas_call x0 -> x1, Pallas kernels: none -> 2.07 us  [per_device(): pl.pallas_call(finish, out_shape=(jax.ShapeDtypeStruct((1,), F32), jax.Sh...]
    pallas_call x1, Pallas kernels: 52.6 us -> 51.1 us  [per_device(): pl.pallas_call(kernel, out_shape=(jax.ShapeDtypeStruct((1, 128), F32), ja...]
where the time goes in v2:
time: 54 us; the launch traced here: 53.9 us
  Pallas kernels  53.2 us (99%)
  between operations  0.64 us (1%)
    pallas_call x1, Pallas kernels, per_device(): pl.pallas_call(kernel, out_shape=(jax.ShapeDtypeStruct((1, 128), F32), ja...  51.1 us
    pallas_call x1, Pallas kernels, per_device(): pl.pallas_call(finish, out_shape=(jax.ShapeDtypeStruct((1,), F32), jax.Sh...  2.07 us

profile of v2, /device:TPU:1, one launch (start us, length us, event | category | flops | bytes accessed | tf_op | source)
XLA Modules:
  0.0 53.9 jit_solution(6528163680035188383)
XLA Ops:
  0.6 51.1 %relations.1 = (f32[1,128]{1,0:T(1,128)}, bf16[128,1536]{1,0:T(8,128)(2,1)}, bf16[2,3,2,2,48,128]{5,4,3,2,1,0:T(8,128)(2,1)}) custom-call(bf16[128,2048]{1,0:T(8,128)(2,1)} %bitcast.4, bf16[128,2048]{1,0:T(8,128)(2,1)} %bitcast.5, bf16[128,1536]{1,0:T(8,128)(2,1)} %bitcast.6, bf16[1536,768]{1,0:T(8,128)(2,1)} %wq.1, bf16[1536,768]{1,0:T(8,128)(2,1)} %wk.1, ...), custom_call_target="tpu_custom_call" | custom-call | tf_op jit(solution)/shard_map/relations/pallas_call | solution.py:549
  51.8 2.1 %finish.1 = (f32[1]{0:T(128)}, bf16[128,1536]{1,0:T(8,128)(2,1)}, f32[96,768]{1,0:T(8,128)}, f32[96,768]{1,0:T(8,128)}) custom-call(f32[1,128]{1,0:T(1,128)} %get-tuple-element.11.loss, bf16[128,1536]{1,0:T(8,128)(2,1)} %get-tuple-element.12.hidden_grad, bf16[2,3,2,2,48,128]{5,4,3,2,1,0:T(8,128)(2,1)} %get-tuple-element.13.terms), custom_call_target="tpu_custom_call" | custom-call | tf_op jit(solution)/shard_map/finish/pallas_call | solution.py:572

commit v3 on v2

v3 whole, which is shorter than its diff:
```python
import math

import jax
import jax.numpy as jnp
from jax import lax
from jax.experimental import pallas as pl
from jax.experimental.pallas import tpu as pltpu
from jax.sharding import PartitionSpec as P

H = 16
TDH = 128
SDH = 48
DOCS = 8
ROWS = 128
SLOTS = 256
TAIL = 64
DS = 1536
TW = H * TDH
SW = H * SDH
LOSS_SCALE = 1048576.0
MASKED = -1e30
LOG2E = math.log2(math.e)
BF = jnp.bfloat16
F32 = jnp.float32
MESH = pl.DeviceIdType.MESH

CHUNKS = 3
PARTS = 3
FIRST_AXIS = (("x", "y", "x"), ("y", "x", "y"), ("z", "z", "x"))
READY = (5, 10, 15)
EXTENT = {"xl": 2, "z": 4, "y": 4, "xh": 2}
UNIT = (16, 128)
GROUPS_OF_HEADS = ((0, 4), (4, 8), (8, 12), (12, 14), (14, 16))


def dims_of(axis):
    return ("xl", "xh") if axis == "x" else (axis,)


def left_after(axis):
    return tuple(d for d in ("xl", "z", "y", "xh") if d not in dims_of(axis))


def extent(dims):
    return tuple(EXTENT[d] for d in dims)


def kernel(
    tq,
    tk,
    hid,
    wq,
    wk,
    lengths,
    out_loss,
    out_hidden,
    out_terms,
    T,
    Ttail,
    Hd,
    Htail,
    HdT,
    Wown,
    Woth,
    S,
    X,
    E,
    G,
    Gb,
    GX,
    GT,
    Wb,
    agbuf,
    final,
    lossb,
    lossr,
    spare,
    *rest,
):
    pieces = CHUNKS * PARTS
    terms_of, halved, in_line, in_plane = (
        rest[i * pieces : (i + 1) * pieces] for i in range(4)
    )
    loc, tail_s, tail_r, rs_s, rs_r, ag_s, ag_r, loss_s, loss_r = rest[4 * pieces :]

    dp = lax.axis_index("dp")
    ctx = lax.axis_index("ctx")
    y, xh = lax.div(dp, 2), lax.rem(dp, 2)
    core = lax.rem(ctx, 2)
    k = lax.div(ctx, 2)
    z, xl = lax.rem(k, 4), lax.div(k, 4)
    x = xh * 2 + xl
    coords = {"x": x, "y": y, "z": z}

    def device(x_, y_, z_, core_):
        return {"dp": y_ * 2 + lax.div(x_, 2), "ctx": (lax.rem(x_, 2) * 4 + z_) * 2 + core_}

    def along(axis, j):
        c = dict(coords)
        c[axis] = lax.rem(c[axis] + j, 4)
        return device(c["x"], c["y"], c["z"], core), c[axis]

    pair = {"dp": dp, "ctx": k * 2 + 1 - core}
    is0, is1 = core == 0, core == 1
    has_next, has_prev = k < 7, k > 0
    sends = jnp.logical_and(is1, has_next)

    mine = pl.ds(pl.multiple_of(core * ROWS, ROWS), ROWS)
    theirs = pl.ds(pl.multiple_of((1 - core) * ROWS, ROWS), ROWS)
    own_hidden = pltpu.make_async_copy(hid, Hd.at[mine], loc.at[0])
    own_hidden.start()

    def by_core(first, second, dst, sem):
        def go(src):
            def start():
                pltpu.make_async_copy(src, dst, sem).start()

            return start

        pl.when(is0)(go(first))
        pl.when(is1)(go(second))
        return pltpu.make_async_copy(first, dst, sem)

    w_own = by_core(wq, wk, Wown, loc.at[1])
    own_t = by_core(tq, tk, T.at[mine], loc.at[2])
    w_oth = by_core(wk, wq, Woth, loc.at[3])

    barrier = pltpu.get_barrier_semaphore()

    def hail(device_id):
        pl.semaphore_signal(barrier, inc=1, device_id=device_id, device_id_type=MESH)

    hail(pair)
    for axis in ("x", "y", "z"):
        for j in (1, 2, 3):
            hail(along(axis, j)[0])

    @pl.when(sends)
    def _():
        hail({"dp": dp, "ctx": k * 2 + 2})
        hail({"dp": dp, "ctx": k * 2 + 3})

    @pl.when(has_prev)
    def _():
        hail({"dp": dp, "ctx": k * 2 - 1})

    pl.semaphore_wait(
        barrier, 10 + jnp.where(sends, 2, 0) + jnp.where(has_prev, 1, 0)
    )

    pending = []

    def copy_of(src, dst, send_sem, recv_sem, device_id):
        return pltpu.make_async_remote_copy(
            src_ref=src,
            dst_ref=dst,
            send_sem=send_sem,
            recv_sem=recv_sem,
            device_id=device_id,
            device_id_type=MESH,
        )

    def when(cond, act):
        if cond is None:
            act()
        else:
            pl.when(cond)(act)

    def remote(src, dst, send_sem, recv_sem, device_id, cond=None):
        when(cond, copy_of(src, dst, send_sem, recv_sem, device_id).start)

    def sent(like, send_sem, cond=None):
        pending.append((copy_of(like, like, send_sem, send_sem, pair), cond))

    def arrived(dst, recv_sem, cond=None):
        when(cond, copy_of(dst, dst, recv_sem, recv_sem, pair).wait_recv)

    last = pl.ds(ROWS - TAIL, TAIL)
    half = DS // 2
    remote(hid, Hd.at[mine], tail_s.at[0], tail_r.at[0], pair)
    sent(Hd.at[mine], tail_s.at[0])
    for c in range(2):
        cols = pl.ds(c * half, half)
        remote(
            hid.at[last, cols],
            Htail.at[:, cols],
            tail_s.at[1],
            tail_r.at[1],
            {"dp": dp, "ctx": k * 2 + 2 + c},
            sends,
        )
    sent(Htail, tail_s.at[1], sends)
    remote(tk, T.at[mine], tail_s.at[2], tail_r.at[2], pair, is0)
    remote(tq, T.at[mine], tail_s.at[2], tail_r.at[2], pair, is1)
    sent(T.at[mine], tail_s.at[2])
    for q, (h0, h1) in enumerate(GROUPS_OF_HEADS):
        cols = pl.ds(TDH * h0, TDH * (h1 - h0))
        for c, src in enumerate((tq, tk)):
            remote(
                src.at[last, cols],
                Ttail.at[:, cols],
                tail_s.at[3],
                tail_r.at[3 + q],
                {"dp": dp, "ctx": k * 2 + 2 + c},
                sends,
            )
    sent(T.at[mine], tail_s.at[3], sends)

    start = jnp.int32(0)
    end = jnp.int32(0)
    count = jnp.int32(0)
    for i in range(DOCS):
        value = lengths[0, i]
        start = start + jnp.where(i < k, value, 0)
        end = end + jnp.where(i <= k, value, 0)
        count = count + value
    lo = end - SLOTS * k
    hi = start - SLOTS * (k - 1)
    mean_over = 1.0 / (H * jnp.full((1, 128), count, jnp.int32).astype(F32))
    coefficient = LOSS_SCALE * mean_over

    def slot(shape, first):
        return lax.broadcasted_iota(jnp.int32, shape, 0) + first

    def tail_mask(width):
        return slot((TAIL, width), SLOTS - TAIL) >= hi

    own_hidden.wait()
    w_own.wait()
    arrived(Hd.at[theirs], tail_r.at[0])
    for r in range(0, SLOTS, 128):
        S[r : r + 128, :] = jnp.dot(
            Hd[r : r + 128, :], Wown[...], preferred_element_type=F32
        ).astype(BF)
    my_half = Htail.at[:, pl.ds(pl.multiple_of(core * half, half), half)]
    arrived(my_half, tail_r.at[1], has_prev)
    remote(my_half, my_half, tail_s.at[4], tail_r.at[11], pair, has_prev)
    sent(my_half, tail_s.at[4], has_prev)
    other_half = Htail.at[:, pl.ds(pl.multiple_of((1 - core) * half, half), half)]
    arrived(other_half, tail_r.at[11], has_prev)
    tail_rows = slice(SLOTS - TAIL, SLOTS)
    projected = jnp.dot(Htail[...], Wown[...], preferred_element_type=F32).astype(BF)
    S[tail_rows, :] = jnp.where(tail_mask(SW), projected, S[tail_rows, :])
    Hd[tail_rows, :] = jnp.where(tail_mask(DS), Htail[...], Hd[tail_rows, :])
    for r in range(0, DS, 128):
        HdT[r : r + 128, :] = Hd[:, r : r + 128].T

    own_t.wait()
    arrived(T.at[theirs], tail_r.at[2])

    row_slot = lax.broadcasted_iota(jnp.int32, (SLOTS, 128), 0)
    row_lane = lax.broadcasted_iota(jnp.int32, (SLOTS, 128), 1)
    row_bad = jnp.logical_and(row_slot >= lo, row_slot < hi)
    row_bias = jnp.where(row_bad, MASKED, 0.0)
    bias_tile = jnp.where(row_lane == 0, row_bias, 0.0).astype(BF)
    one_tile = jnp.where(row_lane == 0, 1.0, 0.0).astype(BF)
    bias_all = row_bias.astype(BF)
    rate = []
    for cb in range(2):
        lane_slot = lax.broadcasted_iota(jnp.int32, (1, 128), 1) + 128 * cb
        good = jnp.logical_or(lane_slot < lo, lane_slot >= hi)
        rate.append(jnp.where(good, coefficient, 0.0))
    ct = LOG2E / math.sqrt(TDH)
    cs = LOG2E / math.sqrt(SDH)
    nt = (((1,), (1,)), ((), ()))

    G[...] = jnp.zeros_like(G)

    def probabilities(scores, factor, rate_here):
        high = jnp.max(scores, axis=0, keepdims=True)
        rel = (scores - high) * factor
        raw = jnp.exp2(rel)
        total = jnp.sum(raw, axis=0, keepdims=True)
        return rel, raw * (rate_here / total), jnp.log2(total)

    def student_tiles(h):
        first = SDH * h
        a, b = first // 128, (first + SDH - 1) // 128
        width = (b - a + 1) * 128
        cols = slice(128 * a, 128 * a + width)
        st = S[:, cols]
        lane = lax.broadcasted_iota(jnp.int32, (SLOTS, width), 1) + 128 * a
        inside = jnp.logical_and(lane >= first, lane < first + SDH)
        free = 128 * a if first > 128 * a else 128 * a + width - 1
        return cols, st, jnp.where(inside, st, jnp.zeros_like(st)), lane == free

    def scores(h):
        th = T[:, TDH * h : TDH * (h + 1)]
        X[h % 2] = lax.dot_general(
            jnp.concatenate([th, bias_tile], axis=1),
            jnp.concatenate([th, one_tile], axis=1),
            nt,
            preferred_element_type=F32,
        )
        _, st, picked, free = student_tiles(h)
        bias = jnp.concatenate([bias_all] * (st.shape[1] // 128), axis=1)
        X[2 + h % 2] = lax.dot_general(
            jnp.where(free, bias, picked),
            jnp.where(free, jnp.ones_like(st), st),
            nt,
            preferred_element_type=F32,
        )

    def softmaxes(h, loss):
        for cb in range(2):
            block = slice(128 * cb, 128 * (cb + 1))
            rel_t, et, log_t = probabilities(X[h % 2, :, block], ct, rate[cb])
            rel_s, es, log_s = probabilities(X[2 + h % 2, :, block], cs, rate[cb])
            E[h % 2, :, block] = es - et
            loss = loss + jnp.sum(et * (rel_t - rel_s), axis=0, keepdims=True)
            loss = loss - rate[cb] * (log_t - log_s)
        return loss

    def weigh(h):
        e, w = E.at[h % 2], Wb.at[h % 2]
        cross = e[:128, 128:] + e[128:, :128].T
        for b in range(2):
            block = slice(128 * b, 128 * (b + 1))
            square = e[block, block]
            w[block, block] = (square + square.T).astype(BF)
        w[:128, 128:] = cross.astype(BF)
        w[128:, :128] = cross.T.astype(BF)

    def gradient(h):
        cols, _, picked, _ = student_tiles(h)
        G[:, cols] += jnp.dot(Wb[h % 2], picked, preferred_element_type=F32)

    def at_peer(dims, place):
        index = []
        for d in dims:
            if d in ("xl", "xh"):
                at = place.get("x")
                index.append(
                    slice(None) if at is None else lax.rem(at, 2) if d == "xl" else lax.div(at, 2)
                )
            else:
                index.append(place.get(d, slice(None)))
        return tuple(index)

    def peer_of(offsets):
        place = {a: lax.rem(coords[a] + j, 4) for a, j in offsets.items()}
        full = dict(coords, **place)
        return device(full["x"], full["y"], full["z"], core), place

    ALL_DIMS = ("xl", "z", "y", "xh")

    def send_line(c, p):
        axis, n = FIRST_AXIS[c][p], c * PARTS + p
        for j in (2, 1, 3):
            peer, place = peer_of({axis: j})
            remote(
                terms_of[n].at[at_peer(ALL_DIMS, place)],
                in_line[n].at[j - 1],
                rs_s.at[2 * n],
                rs_r.at[2 * n],
                peer,
            )
        sent(in_line[n], rs_s.at[2 * n])

    def sum_line(c, p):
        axis, n = FIRST_AXIS[c][p], c * PARTS + p
        own = terms_of[n].at[at_peer(ALL_DIMS, {axis: coords[axis]})]
        arrived(in_line[n], rs_r.at[2 * n])
        total = own[...].astype(F32)
        for j in range(3):
            total = total + in_line[n][j].astype(F32)
        halved[n][...] = total.astype(BF)

    def send_plane(c, p):
        axis, n = FIRST_AXIS[c][p], c * PARTS + p
        u, v = (a for a in ("x", "y", "z") if a != axis)
        for ju in (2, 1, 3, 0):
            for jv in (2, 1, 3, 0):
                if ju or jv:
                    peer, place = peer_of({u: ju, v: jv})
                    remote(
                        halved[n].at[at_peer(left_after(axis), place)],
                        in_plane[n].at[ju * 4 + jv - 1],
                        rs_s.at[2 * n + 1],
                        rs_r.at[2 * n + 1],
                        peer,
                    )
        sent(in_plane[n], rs_s.at[2 * n + 1])

    def sum_plane(c, p):
        axis, n = FIRST_AXIS[c][p], c * PARTS + p
        place = {a: coords[a] for a in ("x", "y", "z") if a != axis}
        arrived(in_plane[n], rs_r.at[2 * n + 1])
        total = halved[n][at_peer(left_after(axis), place)].astype(F32)
        for j in range(15):
            total = total + in_plane[n][j].astype(F32)
        final[c, 16 * p : 16 * (p + 1)] = total.astype(BF)

    def after_line(c):
        for p in range(PARTS):
            sum_line(c, p)
        for p in range(PARTS):
            send_plane(c, p)

    def after_plane(c):
        for p in range(PARTS):
            sum_plane(c, p)
        send_final(c)

    def chunk_terms(c):
        cols = slice(256 * c, 256 * (c + 1))
        Gb[:, cols] = (G[:, cols] * (1.0 / math.sqrt(SDH))).astype(BF)
        for xl_ in range(2):
            terms = (
                jnp.dot(HdT[768 * xl_ : 768 * (xl_ + 1), :], Gb[:, cols], preferred_element_type=F32)
                .astype(BF)
                .reshape(4, 4, PARTS, 16, 256)
            )
            for p in range(PARTS):
                for xh_ in range(2):
                    terms_of[c * PARTS + p][xl_, :, :, xh_] = terms[
                        :, :, p, :, 128 * xh_ : 128 * (xh_ + 1)
                    ]
        for p in range(PARTS):
            send_line(c, p)

    yl = lax.rem(y, 2)
    goal = lax.div(y, 2)

    own_block = core * 4 + yl * 2 + xh

    def send_final(c):
        for j in range(8):
            remote(
                final.at[c],
                agbuf.at[c, own_block],
                ag_s.at[c],
                ag_r.at[c],
                {"dp": lax.rem(dp + j, 8), "ctx": k * 2 + goal},
                None if j else core != goal,
            )
        sent(spare, ag_s.at[c], core == goal)
        sent(agbuf.at[c], ag_s.at[c], core != goal)

        @pl.when(core == goal)
        def _():
            agbuf[c, own_block] = final[c]

    loss = jnp.zeros((1, 128), F32)
    def group_arrives(q):
        h0, h1 = GROUPS_OF_HEADS[q]
        cols = slice(TDH * h0, TDH * h1)
        arrived(Ttail.at[:, cols], tail_r.at[3 + q], has_prev)
        T[tail_rows, cols] = jnp.where(
            tail_mask(TDH * (h1 - h0)), Ttail[:, cols], T[tail_rows, cols]
        )

    starts = [h0 for h0, _ in GROUPS_OF_HEADS]
    group_arrives(0)
    scores(0)
    for h in range(H + 1):
        if h + 1 in starts:
            group_arrives(starts.index(h + 1))
        if h + 1 < H:
            scores(h + 1)
        if h:
            gradient(h - 1)
        if h < H:
            loss = softmaxes(h, loss)
            weigh(h)
        if h - 1 in READY:
            chunk_terms(READY.index(h - 1))

    remote(Gb.at[theirs], GX, tail_s.at[5], tail_r.at[8], pair)
    sent(GX, tail_s.at[5])
    remote(
        Gb.at[tail_rows],
        GT.at[core],
        tail_s.at[6],
        tail_r.at[9 + core],
        {"dp": dp, "ctx": k * 2 - 1},
        has_prev,
    )
    sent(GT.at[0], tail_s.at[6], has_prev)
    lossb[0] = jnp.broadcast_to(loss, (8, 128))
    for j in (1, 2, 3):
        remote(lossb.at[0], lossr.at[j - 1], loss_s.at[0], loss_r.at[0], along("z", j)[0])
    sent(lossr.at[0:3], loss_s.at[0])

    after_line(0)

    w_oth.wait()
    arrived(GX, tail_r.at[8])
    for c in range(2):
        arrived(GT.at[c], tail_r.at[9 + c], sends)
    rows = slice(ROWS - TAIL, ROWS)
    lent = slot((TAIL, SW), SLOTS - TAIL - ROWS + core * ROWS) >= lo
    zero = jnp.zeros((TAIL, SW), BF)
    keep = jnp.full((TAIL, SW), k, jnp.int32) < 7
    own_low = Gb[pl.ds(pl.multiple_of(core * ROWS, ROWS), ROWS - TAIL), :]
    own_high = Gb[pl.ds(pl.multiple_of(core * ROWS + ROWS - TAIL, TAIL), TAIL), :]
    own_high = jnp.where(lent, jnp.where(keep, GT[1], zero), own_high)
    GX[rows, :] = jnp.where(lent, jnp.where(keep, GT[0], zero), GX[rows, :])
    own_rows = jnp.concatenate([own_low, own_high], axis=0)
    for r in range(0, DS, 512):
        out_hidden[:, r : r + 512] = (
            lax.dot_general(own_rows, Wown[r : r + 512, :], nt, preferred_element_type=F32)
            + lax.dot_general(GX[...], Woth[r : r + 512, :], nt, preferred_element_type=F32)
        ).astype(BF)

    after_line(1)
    after_plane(0)

    arrived(lossr.at[0:3], loss_r.at[0])
    lossb[1] = lossb[0] + lossr[0] + lossr[1] + lossr[2]
    x_other = xh * 2 + 1 - xl
    remote(lossb.at[1], lossr.at[3], loss_s.at[1], loss_r.at[1], device(x_other, y, z, core))
    sent(lossr.at[3], loss_s.at[1])

    after_line(2)
    after_plane(1)

    arrived(lossr.at[3], loss_r.at[1])
    lossb[2] = lossb[1] + lossr[3]
    remote(lossb.at[2], lossr.at[4], loss_s.at[2], loss_r.at[2], pair)
    sent(lossr.at[4], loss_s.at[2])

    after_plane(2)

    arrived(lossr.at[4], loss_r.at[2])
    loss_total = lossb[2] + lossr[4]
    out_loss[...] = jnp.broadcast_to(
        jnp.sum(loss_total[:1], axis=1, keepdims=True) * (math.log(2.0) / LOSS_SCALE), (1, 128)
    )

    for c in range(CHUNKS):
        arrived(spare, ag_r.at[c], core == goal)
        arrived(agbuf.at[c], ag_r.at[c], core != goal)
        out_terms[c] = agbuf[c]

    for copy, cond in pending:
        if cond is None:
            copy.wait_send()
        else:
            pl.when(cond)(copy.wait_send)


def finish(loss, hidden_grad, terms, out_loss, out_hidden, out_wq, out_wk):
    out_loss[0] = loss[0, 0]
    out_hidden[...] = hidden_grad[...]
    for r, out in enumerate((out_wq, out_wk)):
        for c in range(CHUNKS):
            for yl in range(2):
                for xh in range(2):
                    at = 256 * c + 128 * xh
                    block = terms[c, r * 4 + yl * 2 + xh]
                    out[48 * yl : 48 * (yl + 1), at : at + 128] = block.astype(F32)


def per_device(teacher_query, teacher_key, student_hidden, weight_query, weight_key, doc_lengths):
    scratch = [
        pltpu.VMEM((SLOTS, TW), BF),
        pltpu.VMEM((TAIL, TW), BF),
        pltpu.VMEM((SLOTS, DS), BF),
        pltpu.VMEM((TAIL, DS), BF),
        pltpu.VMEM((DS, SLOTS), BF),
        pltpu.VMEM((DS, SW), BF),
        pltpu.VMEM((DS, SW), BF),
        pltpu.VMEM((SLOTS, SW), BF),
        pltpu.VMEM((4, SLOTS, SLOTS), F32),
        pltpu.VMEM((2, SLOTS, SLOTS), F32),
        pltpu.VMEM((SLOTS, SW), F32),
        pltpu.VMEM((SLOTS, SW), BF),
        pltpu.VMEM((ROWS, SW), BF),
        pltpu.VMEM((2, TAIL, SW), BF),
        pltpu.VMEM((2, SLOTS, SLOTS), BF),
        pltpu.VMEM((CHUNKS, 8, 48, 128), BF),
        pltpu.VMEM((CHUNKS, 48, 128), BF),
        pltpu.VMEM((3, 8, 128), F32),
        pltpu.VMEM((5, 8, 128), F32),
        pltpu.VMEM((7, 48, 128), BF),
    ]
    firsts = [axis for axes in FIRST_AXIS for axis in axes]
    for _ in firsts:
        scratch.append(pltpu.VMEM(extent(("xl", "z", "y", "xh")) + UNIT, BF))
    for axis in firsts:
        scratch.append(pltpu.VMEM(extent(left_after(axis)) + UNIT, BF))
    for axis in firsts:
        scratch.append(pltpu.VMEM((3,) + extent(left_after(axis)) + UNIT, BF))
    for _ in firsts:
        scratch.append(pltpu.VMEM((15,) + UNIT, BF))
    dma = pltpu.SemaphoreType.DMA
    scratch += [
        dma((4,)),
        dma((7,)),
        dma((12,)),
        dma((18,)),
        dma((18,)),
        dma((3,)),
        dma((3,)),
        dma((3,)),
        dma((3,)),
    ]
    vmem = pl.BlockSpec(memory_space=pltpu.VMEM)
    anywhere = pl.BlockSpec(memory_space=pl.ANY)
    loss, hidden_grad, terms = pl.pallas_call(
        kernel,
        out_shape=(
            jax.ShapeDtypeStruct((1, 128), F32),
            jax.ShapeDtypeStruct((ROWS, DS), BF),
            jax.ShapeDtypeStruct((CHUNKS, 8, 48, 128), BF),
        ),
        in_specs=[anywhere] * 5 + [pl.BlockSpec(memory_space=pltpu.SMEM)],
        out_specs=(vmem, vmem, vmem),
        scratch_shapes=scratch,
        compiler_params=pltpu.CompilerParams(
            collective_id=0, has_side_effects=True, vmem_limit_bytes=56 * 1024 * 1024
        ),
        name="relations",
    )(
        teacher_query[0],
        teacher_key[0],
        student_hidden[0],
        weight_query,
        weight_key,
        doc_lengths,
    )
    smem = pl.BlockSpec(memory_space=pltpu.SMEM)
    loss, hidden_grad, grad_wq, grad_wk = pl.pallas_call(
        finish,
        out_shape=(
            jax.ShapeDtypeStruct((1,), F32),
            jax.ShapeDtypeStruct((ROWS, DS), BF),
            jax.ShapeDtypeStruct((96, SW), F32),
            jax.ShapeDtypeStruct((96, SW), F32),
        ),
        in_specs=[smem, vmem, vmem],
        out_specs=(smem, vmem, vmem, vmem),
        name="finish",
    )(loss, hidden_grad, terms)
    return loss, hidden_grad[None], grad_wq, grad_wk


def solution(mesh):
    in_specs = (
        P("dp", "ctx", None),
        P("dp", "ctx", None),
        P("dp", "ctx", None),
        P(),
        P(),
        P("dp", None),
    )
    out_specs = (P("dp"), P("dp", "ctx", None), P("ctx", None), P("ctx", None))
    return jax.shard_map(
        per_device, mesh=mesh, in_specs=in_specs, out_specs=out_specs, check_vma=False
    )
```

time: 54 us -> 51.1 us (0.946)
  Pallas kernels: 53.2 us -> 50.4 us
    pallas_call x1, Pallas kernels: 51.1 us -> 48.3 us  [per_device(): pl.pallas_call(kernel, out_shape=(jax.ShapeDtypeStruct((1, 128), F32), ja...]
where the time goes in v3:
time: 51.1 us; the launch traced here: 51 us
  Pallas kernels  50.4 us (99%)
  between operations  0.64 us (1%)
    pallas_call x1, Pallas kernels, per_device(): pl.pallas_call(kernel, out_shape=(jax.ShapeDtypeStruct((1, 128), F32), ja...  48.3 us
    pallas_call x1, Pallas kernels, per_device(): pl.pallas_call(finish, out_shape=(jax.ShapeDtypeStruct((1,), F32), jax.Sh...  2.07 us

profile of v3, /device:TPU:1, one launch (start us, length us, event | category | flops | bytes accessed | tf_op | source)
XLA Modules:
  0.0 51.0 jit_solution(14715588911126609064)
XLA Ops:
  0.6 48.3 %relations.1 = (f32[1,128]{1,0:T(1,128)}, bf16[128,1536]{1,0:T(8,128)(2,1)}, bf16[3,8,48,128]{3,2,1,0:T(8,128)(2,1)}) custom-call(bf16[128,2048]{1,0:T(8,128)(2,1)} %bitcast.4, bf16[128,2048]{1,0:T(8,128)(2,1)} %bitcast.5, bf16[128,1536]{1,0:T(8,128)(2,1)} %bitcast.6, bf16[1536,768]{1,0:T(8,128)(2,1)} %wq.1, bf16[1536,768]{1,0:T(8,128)(2,1)} %wk.1, ...), custom_call_target="tpu_custom_call" | custom-call | tf_op jit(solution)/shard_map/relations/pallas_call | solution.py:601
  48.9 2.1 %finish.1 = (f32[1]{0:T(128)}, bf16[128,1536]{1,0:T(8,128)(2,1)}, f32[96,768]{1,0:T(8,128)}, f32[96,768]{1,0:T(8,128)}) custom-call(f32[1,128]{1,0:T(1,128)} %get-tuple-element.11.loss, bf16[128,1536]{1,0:T(8,128)(2,1)} %get-tuple-element.12.hidden_grad, bf16[3,8,48,128]{3,2,1,0:T(8,128)(2,1)} %get-tuple-element.13.terms), custom_call_target="tpu_custom_call" | custom-call | tf_op jit(solution)/shard_map/finish/pallas_call | solution.py:624

commit v4 on v3

--- a/solution.py
+++ b/solution.py
@@ -26,7 +26,7 @@
 
 CHUNKS = 3
 PARTS = 3
-FIRST_AXIS = (("x", "y", "x"), ("y", "x", "y"), ("z", "z", "x"))
+FIRST_AXIS = (("x", "y", "z"), ("x", "y", "z"), ("x", "y", "z"))
 READY = (5, 10, 15)
 EXTENT = {"xl": 2, "z": 4, "y": 4, "xh": 2}
 UNIT = (16, 128)
@@ -466,6 +466,15 @@
         if h - 1 in READY:
             chunk_terms(READY.index(h - 1))
 
+    lossb[0] = jnp.broadcast_to(loss, (8, 128))
+    for j in (1, 2, 3):
+        remote(lossb.at[0], lossr.at[j - 1], loss_s.at[0], loss_r.at[0], along("z", j)[0])
+    sent(lossr.at[0:3], loss_s.at[0])
+
+    after_line(0)
+
+    after_line(1)
+    after_line(2)
     remote(Gb.at[theirs], GX, tail_s.at[5], tail_r.at[8], pair)
     sent(GX, tail_s.at[5])
     remote(
@@ -477,12 +486,22 @@
         has_prev,
     )
     sent(GT.at[0], tail_s.at[6], has_prev)
-    lossb[0] = jnp.broadcast_to(loss, (8, 128))
-    for j in (1, 2, 3):
-        remote(lossb.at[0], lossr.at[j - 1], loss_s.at[0], loss_r.at[0], along("z", j)[0])
-    sent(lossr.at[0:3], loss_s.at[0])
-
-    after_line(0)
+
+    arrived(lossr.at[0:3], loss_r.at[0])
+    lossb[1] = lossb[0] + lossr[0] + lossr[1] + lossr[2]
+    x_other = xh * 2 + 1 - xl
+    remote(lossb.at[1], lossr.at[3], loss_s.at[1], loss_r.at[1], device(x_other, y, z, core))
+    sent(lossr.at[3], loss_s.at[1])
+
+    after_plane(0)
+    after_plane(1)
+
+    arrived(lossr.at[3], loss_r.at[1])
+    lossb[2] = lossb[1] + lossr[3]
+    remote(lossb.at[2], lossr.at[4], loss_s.at[2], loss_r.at[2], pair)
+    sent(lossr.at[4], loss_s.at[2])
+
+    after_plane(2)
 
     w_oth.wait()
     arrived(GX, tail_r.at[8])
@@ -502,25 +521,6 @@
             lax.dot_general(own_rows, Wown[r : r + 512, :], nt, preferred_element_type=F32)
             + lax.dot_general(GX[...], Woth[r : r + 512, :], nt, preferred_element_type=F32)
         ).astype(BF)
-
-    after_line(1)
-    after_plane(0)
-
-    arrived(lossr.at[0:3], loss_r.at[0])
-    lossb[1] = lossb[0] + lossr[0] + lossr[1] + lossr[2]
-    x_other = xh * 2 + 1 - xl
-    remote(lossb.at[1], lossr.at[3], loss_s.at[1], loss_r.at[1], device(x_other, y, z, core))
-    sent(lossr.at[3], loss_s.at[1])
-
-    after_line(2)
-    after_plane(1)
-
-    arrived(lossr.at[3], loss_r.at[1])
-    lossb[2] = lossb[1] + lossr[3]
-    remote(lossb.at[2], lossr.at[4], loss_s.at[2], loss_r.at[2], pair)
-    sent(lossr.at[4], loss_s.at[2])
-
-    after_plane(2)
 
     arrived(lossr.at[4], loss_r.at[2])
     loss_total = lossb[2] + lossr[4]

time: 51.1 us -> 44.7 us (0.87)
  Pallas kernels: 50.4 us -> 43.9 us
    pallas_call x1, Pallas kernels: 48.3 us -> 41.8 us  [per_device(): pl.pallas_call(kernel, out_shape=(jax.ShapeDtypeStruct((1, 128), F32), ja...]
where the time goes in v4:
time: 44.7 us; the launch traced here: 44.5 us
  Pallas kernels  43.9 us (98%)
  between operations  0.64 us (1%)
    pallas_call x1, Pallas kernels, per_device(): pl.pallas_call(kernel, out_shape=(jax.ShapeDtypeStruct((1, 128), F32), ja...  41.8 us
    pallas_call x1, Pallas kernels, per_device(): pl.pallas_call(finish, out_shape=(jax.ShapeDtypeStruct((1,), F32), jax.Sh...  2.07 us

profile of v4, /device:TPU:1, one launch (start us, length us, event | category | flops | bytes accessed | tf_op | source)
XLA Modules:
  0.0 44.5 jit_solution(9068492769132375445)
XLA Ops:
  0.6 41.8 %relations.1 = (f32[1,128]{1,0:T(1,128)}, bf16[128,1536]{1,0:T(8,128)(2,1)}, bf16[3,8,48,128]{3,2,1,0:T(8,128)(2,1)}) custom-call(bf16[128,2048]{1,0:T(8,128)(2,1)} %bitcast.4, bf16[128,2048]{1,0:T(8,128)(2,1)} %bitcast.5, bf16[128,1536]{1,0:T(8,128)(2,1)} %bitcast.6, bf16[1536,768]{1,0:T(8,128)(2,1)} %wq.1, bf16[1536,768]{1,0:T(8,128)(2,1)} %wk.1, ...), custom_call_target="tpu_custom_call" | custom-call | tf_op jit(solution)/shard_map/relations/pallas_call | solution.py:601
  42.5 2.1 %finish.1 = (f32[1]{0:T(128)}, bf16[128,1536]{1,0:T(8,128)(2,1)}, f32[96,768]{1,0:T(8,128)}, f32[96,768]{1,0:T(8,128)}) custom-call(f32[1,128]{1,0:T(1,128)} %get-tuple-element.11.loss, bf16[128,1536]{1,0:T(8,128)(2,1)} %get-tuple-element.12.hidden_grad, bf16[3,8,48,128]{3,2,1,0:T(8,128)(2,1)} %get-tuple-element.13.terms), custom_call_target="tpu_custom_call" | custom-call | tf_op jit(solution)/shard_map/finish/pallas_call | solution.py:624

commit v5 on v4

--- a/solution.py
+++ b/solution.py
@@ -26,8 +26,8 @@
 
 CHUNKS = 3
 PARTS = 3
-FIRST_AXIS = (("x", "y", "z"), ("x", "y", "z"), ("x", "y", "z"))
-READY = (5, 10, 15)
+FIRST_AXIS = ("x", "y", "z")
+TILE_OF_HEAD = {(128 * (t + 1) - 1) // SDH: t for t in range(2 * CHUNKS)}
 EXTENT = {"xl": 2, "z": 4, "y": 4, "xh": 2}
 UNIT = (16, 128)
 GROUPS_OF_HEADS = ((0, 4), (4, 8), (8, 12), (12, 14), (14, 16))
@@ -51,10 +51,11 @@
     hid,
     wq,
     wk,
-    lengths,
+    lengths_in,
     out_loss,
     out_hidden,
     out_terms,
+    lengths,
     T,
     Ttail,
     Hd,
@@ -109,6 +110,8 @@
     theirs = pl.ds(pl.multiple_of((1 - core) * ROWS, ROWS), ROWS)
     own_hidden = pltpu.make_async_copy(hid, Hd.at[mine], loc.at[0])
     own_hidden.start()
+    get_lengths = pltpu.make_async_copy(lengths_in, lengths, loc.at[4])
+    get_lengths.start()
 
     def by_core(first, second, dst, sem):
         def go(src):
@@ -177,8 +180,6 @@
 
     last = pl.ds(ROWS - TAIL, TAIL)
     half = DS // 2
-    remote(hid, Hd.at[mine], tail_s.at[0], tail_r.at[0], pair)
-    sent(Hd.at[mine], tail_s.at[0])
     for c in range(2):
         cols = pl.ds(c * half, half)
         remote(
@@ -190,9 +191,8 @@
             sends,
         )
     sent(Htail, tail_s.at[1], sends)
-    remote(tk, T.at[mine], tail_s.at[2], tail_r.at[2], pair, is0)
-    remote(tq, T.at[mine], tail_s.at[2], tail_r.at[2], pair, is1)
-    sent(T.at[mine], tail_s.at[2])
+    remote(hid, Hd.at[mine], tail_s.at[0], tail_r.at[0], pair)
+    sent(Hd.at[mine], tail_s.at[0])
     for q, (h0, h1) in enumerate(GROUPS_OF_HEADS):
         cols = pl.ds(TDH * h0, TDH * (h1 - h0))
         for c, src in enumerate((tq, tk)):
@@ -205,7 +205,11 @@
                 sends,
             )
     sent(T.at[mine], tail_s.at[3], sends)
-
+    remote(tk, T.at[mine], tail_s.at[2], tail_r.at[2], pair, is0)
+    remote(tq, T.at[mine], tail_s.at[2], tail_r.at[2], pair, is1)
+    sent(T.at[mine], tail_s.at[2])
+
+    get_lengths.wait()
     start = jnp.int32(0)
     end = jnp.int32(0)
     count = jnp.int32(0)
@@ -344,21 +348,23 @@
 
     ALL_DIMS = ("xl", "z", "y", "xh")
 
-    def send_line(c, p):
-        axis, n = FIRST_AXIS[c][p], c * PARTS + p
+    def send_line(c, p, half_):
+        axis, n = FIRST_AXIS[p], c * PARTS + p
         for j in (2, 1, 3):
             peer, place = peer_of({axis: j})
-            remote(
-                terms_of[n].at[at_peer(ALL_DIMS, place)],
-                in_line[n].at[j - 1],
-                rs_s.at[2 * n],
-                rs_r.at[2 * n],
-                peer,
-            )
+            index = at_peer(ALL_DIMS, place)
+            dst = in_line[n].at[j - 1]
+            if axis == "x":
+                cond = lax.div(place["x"], 2) == half_
+            else:
+                cond = None
+                index = index[:3] + (half_,)
+                dst = dst.at[:, :, half_]
+            remote(terms_of[n].at[index], dst, rs_s.at[2 * n], rs_r.at[2 * n], peer, cond)
+
+    def sum_line(c, p):
+        axis, n = FIRST_AXIS[p], c * PARTS + p
         sent(in_line[n], rs_s.at[2 * n])
-
-    def sum_line(c, p):
-        axis, n = FIRST_AXIS[c][p], c * PARTS + p
         own = terms_of[n].at[at_peer(ALL_DIMS, {axis: coords[axis]})]
         arrived(in_line[n], rs_r.at[2 * n])
         total = own[...].astype(F32)
@@ -367,7 +373,7 @@
         halved[n][...] = total.astype(BF)
 
     def send_plane(c, p):
-        axis, n = FIRST_AXIS[c][p], c * PARTS + p
+        axis, n = FIRST_AXIS[p], c * PARTS + p
         u, v = (a for a in ("x", "y", "z") if a != axis)
         for ju in (2, 1, 3, 0):
             for jv in (2, 1, 3, 0):
@@ -383,7 +389,7 @@
         sent(in_plane[n], rs_s.at[2 * n + 1])
 
     def sum_plane(c, p):
-        axis, n = FIRST_AXIS[c][p], c * PARTS + p
+        axis, n = FIRST_AXIS[p], c * PARTS + p
         place = {a: coords[a] for a in ("x", "y", "z") if a != axis}
         arrived(in_plane[n], rs_r.at[2 * n + 1])
         total = halved[n][at_peer(left_after(axis), place)].astype(F32)
@@ -394,30 +400,31 @@
     def after_line(c):
         for p in range(PARTS):
             sum_line(c, p)
-        for p in range(PARTS):
-            send_plane(c, p)
+            if c:
+                send_plane(c, p)
+        if c == 0:
+            for p in range(PARTS):
+                send_plane(c, p)
 
     def after_plane(c):
         for p in range(PARTS):
             sum_plane(c, p)
         send_final(c)
 
-    def chunk_terms(c):
-        cols = slice(256 * c, 256 * (c + 1))
+    def tile_terms(t):
+        c, half_ = t // 2, t % 2
+        cols = slice(128 * t, 128 * (t + 1))
         Gb[:, cols] = (G[:, cols] * (1.0 / math.sqrt(SDH))).astype(BF)
         for xl_ in range(2):
             terms = (
                 jnp.dot(HdT[768 * xl_ : 768 * (xl_ + 1), :], Gb[:, cols], preferred_element_type=F32)
                 .astype(BF)
-                .reshape(4, 4, PARTS, 16, 256)
+                .reshape(4, 4, PARTS, 16, 128)
             )
             for p in range(PARTS):
-                for xh_ in range(2):
-                    terms_of[c * PARTS + p][xl_, :, :, xh_] = terms[
-                        :, :, p, :, 128 * xh_ : 128 * (xh_ + 1)
-                    ]
+                terms_of[c * PARTS + p][xl_, :, :, half_] = terms[:, :, p]
         for p in range(PARTS):
-            send_line(c, p)
+            send_line(c, p, half_)
 
     yl = lax.rem(y, 2)
     goal = lax.div(y, 2)
@@ -463,8 +470,8 @@
         if h < H:
             loss = softmaxes(h, loss)
             weigh(h)
-        if h - 1 in READY:
-            chunk_terms(READY.index(h - 1))
+        if h - 1 in TILE_OF_HEAD:
+            tile_terms(TILE_OF_HEAD[h - 1])
 
     lossb[0] = jnp.broadcast_to(loss, (8, 128))
     for j in (1, 2, 3):
@@ -473,8 +480,6 @@
 
     after_line(0)
 
-    after_line(1)
-    after_line(2)
     remote(Gb.at[theirs], GX, tail_s.at[5], tail_r.at[8], pair)
     sent(GX, tail_s.at[5])
     remote(
@@ -487,21 +492,13 @@
     )
     sent(GT.at[0], tail_s.at[6], has_prev)
 
+    after_line(1)
+    after_line(2)
     arrived(lossr.at[0:3], loss_r.at[0])
     lossb[1] = lossb[0] + lossr[0] + lossr[1] + lossr[2]
     x_other = xh * 2 + 1 - xl
     remote(lossb.at[1], lossr.at[3], loss_s.at[1], loss_r.at[1], device(x_other, y, z, core))
     sent(lossr.at[3], loss_s.at[1])
-
-    after_plane(0)
-    after_plane(1)
-
-    arrived(lossr.at[3], loss_r.at[1])
-    lossb[2] = lossb[1] + lossr[3]
-    remote(lossb.at[2], lossr.at[4], loss_s.at[2], loss_r.at[2], pair)
-    sent(lossr.at[4], loss_s.at[2])
-
-    after_plane(2)
 
     w_oth.wait()
     arrived(GX, tail_r.at[8])
@@ -522,6 +519,16 @@
             + lax.dot_general(GX[...], Woth[r : r + 512, :], nt, preferred_element_type=F32)
         ).astype(BF)
 
+    after_plane(0)
+    after_plane(1)
+
+    arrived(lossr.at[3], loss_r.at[1])
+    lossb[2] = lossb[1] + lossr[3]
+    remote(lossb.at[2], lossr.at[4], loss_s.at[2], loss_r.at[2], pair)
+    sent(lossr.at[4], loss_s.at[2])
+
+    after_plane(2)
+
     arrived(lossr.at[4], loss_r.at[2])
     loss_total = lossb[2] + lossr[4]
     out_loss[...] = jnp.broadcast_to(
@@ -554,6 +561,7 @@
 
 def per_device(teacher_query, teacher_key, student_hidden, weight_query, weight_key, doc_lengths):
     scratch = [
+        pltpu.SMEM((1, DOCS), jnp.int32),
         pltpu.VMEM((SLOTS, TW), BF),
         pltpu.VMEM((TAIL, TW), BF),
         pltpu.VMEM((SLOTS, DS), BF),
@@ -575,7 +583,7 @@
         pltpu.VMEM((5, 8, 128), F32),
         pltpu.VMEM((7, 48, 128), BF),
     ]
-    firsts = [axis for axes in FIRST_AXIS for axis in axes]
+    firsts = FIRST_AXIS * CHUNKS
     for _ in firsts:
         scratch.append(pltpu.VMEM(extent(("xl", "z", "y", "xh")) + UNIT, BF))
     for axis in firsts:
@@ -586,7 +594,7 @@
         scratch.append(pltpu.VMEM((15,) + UNIT, BF))
     dma = pltpu.SemaphoreType.DMA
     scratch += [
-        dma((4,)),
+        dma((5,)),
         dma((7,)),
         dma((12,)),
         dma((18,)),
@@ -605,7 +613,7 @@
             jax.ShapeDtypeStruct((ROWS, DS), BF),
             jax.ShapeDtypeStruct((CHUNKS, 8, 48, 128), BF),
         ),
-        in_specs=[anywhere] * 5 + [pl.BlockSpec(memory_space=pltpu.SMEM)],
+        in_specs=[anywhere] * 6,
         out_specs=(vmem, vmem, vmem),
         scratch_shapes=scratch,
         compiler_params=pltpu.CompilerParams(

time: 44.7 us -> 43.3 us (0.969)
  Pallas kernels: 43.9 us -> 42.6 us
    pallas_call x1, Pallas kernels: 41.8 us -> 40.5 us  [per_device(): pl.pallas_call(kernel, out_shape=(jax.ShapeDtypeStruct((1, 128), F32), ja...]
where the time goes in v5:
time: 43.3 us; the launch traced here: 43.2 us
  Pallas kernels  42.6 us (98%)
  between operations  0.64 us (1%)
    pallas_call x1, Pallas kernels, per_device(): pl.pallas_call(kernel, out_shape=(jax.ShapeDtypeStruct((1, 128), F32), ja...  40.5 us
    pallas_call x1, Pallas kernels, per_device(): pl.pallas_call(finish, out_shape=(jax.ShapeDtypeStruct((1,), F32), jax.Sh...  2.07 us

profile of v5, /device:TPU:1, one launch (start us, length us, event | category | flops | bytes accessed | tf_op | source)
XLA Modules:
  0.0 43.2 jit_solution(10857508867664507639)
XLA Ops:
  0.6 40.5 %relations.1 = (f32[1,128]{1,0:T(1,128)}, bf16[128,1536]{1,0:T(8,128)(2,1)}, bf16[3,8,48,128]{3,2,1,0:T(8,128)(2,1)}) custom-call(bf16[128,2048]{1,0:T(8,128)(2,1)} %bitcast.4, bf16[128,2048]{1,0:T(8,128)(2,1)} %bitcast.5, bf16[128,1536]{1,0:T(8,128)(2,1)} %bitcast.6, bf16[1536,768]{1,0:T(8,128)(2,1)} %wq.1, bf16[1536,768]{1,0:T(8,128)(2,1)} %wk.1, ...), custom_call_target="tpu_custom_call" | custom-call | tf_op jit(solution)/shard_map/relations/pallas_call | solution.py:609
  41.1 2.1 %finish.1 = (f32[1]{0:T(128)}, bf16[128,1536]{1,0:T(8,128)(2,1)}, f32[96,768]{1,0:T(8,128)}, f32[96,768]{1,0:T(8,128)}) custom-call(f32[1,128]{1,0:T(1,128)} %get-tuple-element.11.loss, bf16[128,1536]{1,0:T(8,128)(2,1)} %get-tuple-element.12.hidden_grad, bf16[3,8,48,128]{3,2,1,0:T(8,128)(2,1)} %get-tuple-element.13.terms), custom_call_target="tpu_custom_call" | custom-call | tf_op jit(solution)/shard_map/finish/pallas_call | solution.py:632

commit v6 on v5

--- a/solution.py
+++ b/solution.py
@@ -30,7 +30,7 @@
 TILE_OF_HEAD = {(128 * (t + 1) - 1) // SDH: t for t in range(2 * CHUNKS)}
 EXTENT = {"xl": 2, "z": 4, "y": 4, "xh": 2}
 UNIT = (16, 128)
-GROUPS_OF_HEADS = ((0, 4), (4, 8), (8, 12), (12, 14), (14, 16))
+GROUPS_OF_HEADS = ((0, 2), (2, 6), (6, 10), (10, 13), (13, 16))
 
 
 def dims_of(axis):
@@ -236,6 +236,8 @@
         S[r : r + 128, :] = jnp.dot(
             Hd[r : r + 128, :], Wown[...], preferred_element_type=F32
         ).astype(BF)
+    for r in range(0, DS, 128):
+        HdT[r : r + 128, :ROWS] = Hd[:ROWS, r : r + 128].T
     my_half = Htail.at[:, pl.ds(pl.multiple_of(core * half, half), half)]
     arrived(my_half, tail_r.at[1], has_prev)
     remote(my_half, my_half, tail_s.at[4], tail_r.at[11], pair, has_prev)
@@ -245,9 +247,6 @@
     tail_rows = slice(SLOTS - TAIL, SLOTS)
     projected = jnp.dot(Htail[...], Wown[...], preferred_element_type=F32).astype(BF)
     S[tail_rows, :] = jnp.where(tail_mask(SW), projected, S[tail_rows, :])
-    Hd[tail_rows, :] = jnp.where(tail_mask(DS), Htail[...], Hd[tail_rows, :])
-    for r in range(0, DS, 128):
-        HdT[r : r + 128, :] = Hd[:, r : r + 128].T
 
     own_t.wait()
     arrived(T.at[theirs], tail_r.at[2])
@@ -409,7 +408,12 @@
     def after_plane(c):
         for p in range(PARTS):
             sum_plane(c, p)
-        send_final(c)
+            if c == CHUNKS - 1:
+                send_final(c, 16 * p, 16 * (p + 1))
+        if c < CHUNKS - 1:
+            send_final(c, 0, 48)
+        sent(spare, ag_s.at[c], core == goal)
+        sent(agbuf.at[c], ag_s.at[c], core != goal)
 
     def tile_terms(t):
         c, half_ = t // 2, t % 2
@@ -431,22 +435,21 @@
 
     own_block = core * 4 + yl * 2 + xh
 
-    def send_final(c):
-        for j in range(8):
+    def send_final(c, first, stop):
+        rows = pl.ds(first, stop - first)
+        for j in (4, 5, 3, 2, 6, 1, 7, 0):
             remote(
-                final.at[c],
-                agbuf.at[c, own_block],
+                final.at[c, rows],
+                agbuf.at[c, own_block, rows],
                 ag_s.at[c],
                 ag_r.at[c],
                 {"dp": lax.rem(dp + j, 8), "ctx": k * 2 + goal},
                 None if j else core != goal,
             )
-        sent(spare, ag_s.at[c], core == goal)
-        sent(agbuf.at[c], ag_s.at[c], core != goal)
 
         @pl.when(core == goal)
         def _():
-            agbuf[c, own_block] = final[c]
+            agbuf[c, own_block, first:stop] = final[c, first:stop]
 
     loss = jnp.zeros((1, 128), F32)
     def group_arrives(q):
@@ -470,6 +473,10 @@
         if h < H:
             loss = softmaxes(h, loss)
             weigh(h)
+        if h == 2:
+            Hd[tail_rows, :] = jnp.where(tail_mask(DS), Htail[...], Hd[tail_rows, :])
+            for r in range(0, DS, 128):
+                HdT[r : r + 128, ROWS:] = Hd[ROWS:, r : r + 128].T
         if h - 1 in TILE_OF_HEAD:
             tile_terms(TILE_OF_HEAD[h - 1])
 
@@ -499,6 +506,16 @@
     x_other = xh * 2 + 1 - xl
     remote(lossb.at[1], lossr.at[3], loss_s.at[1], loss_r.at[1], device(x_other, y, z, core))
     sent(lossr.at[3], loss_s.at[1])
+
+    after_plane(0)
+    after_plane(1)
+
+    arrived(lossr.at[3], loss_r.at[1])
+    lossb[2] = lossb[1] + lossr[3]
+    remote(lossb.at[2], lossr.at[4], loss_s.at[2], loss_r.at[2], pair)
+    sent(lossr.at[4], loss_s.at[2])
+
+    after_plane(2)
 
     w_oth.wait()
     arrived(GX, tail_r.at[8])
@@ -518,16 +535,6 @@
             lax.dot_general(own_rows, Wown[r : r + 512, :], nt, preferred_element_type=F32)
             + lax.dot_general(GX[...], Woth[r : r + 512, :], nt, preferred_element_type=F32)
         ).astype(BF)
-
-    after_plane(0)
-    after_plane(1)
-
-    arrived(lossr.at[3], loss_r.at[1])
-    lossb[2] = lossb[1] + lossr[3]
-    remote(lossb.at[2], lossr.at[4], loss_s.at[2], loss_r.at[2], pair)
-    sent(lossr.at[4], loss_s.at[2])
-
-    after_plane(2)
 
     arrived(lossr.at[4], loss_r.at[2])
     loss_total = lossb[2] + lossr[4]

time: 43.3 us -> 43 us (level)
  no operation moved by 1% of the time
where the time goes in v6:
time: 43 us; the launch traced here: 42.9 us
  Pallas kernels  42.2 us (98%)
  between operations  0.64 us (1%)
    pallas_call x1, Pallas kernels, per_device(): pl.pallas_call(kernel, out_shape=(jax.ShapeDtypeStruct((1, 128), F32), ja...  40.2 us
    pallas_call x1, Pallas kernels, per_device(): pl.pallas_call(finish, out_shape=(jax.ShapeDtypeStruct((1,), F32), jax.Sh...  2.07 us

profile of v6, /device:TPU:1, one launch (start us, length us, event | category | flops | bytes accessed | tf_op | source)
XLA Modules:
  0.0 42.9 jit_solution(16489409622176585297)
XLA Ops:
  0.6 40.2 %relations.1 = (f32[1,128]{1,0:T(1,128)}, bf16[128,1536]{1,0:T(8,128)(2,1)}, bf16[3,8,48,128]{3,2,1,0:T(8,128)(2,1)}) custom-call(bf16[128,2048]{1,0:T(8,128)(2,1)} %bitcast.4, bf16[128,2048]{1,0:T(8,128)(2,1)} %bitcast.5, bf16[128,1536]{1,0:T(8,128)(2,1)} %bitcast.6, bf16[1536,768]{1,0:T(8,128)(2,1)} %wq.1, bf16[1536,768]{1,0:T(8,128)(2,1)} %wk.1, ...), custom_call_target="tpu_custom_call" | custom-call | tf_op jit(solution)/shard_map/relations/pallas_call | solution.py:616
  40.8 2.1 %finish.1 = (f32[1]{0:T(128)}, bf16[128,1536]{1,0:T(8,128)(2,1)}, f32[96,768]{1,0:T(8,128)}, f32[96,768]{1,0:T(8,128)}) custom-call(f32[1,128]{1,0:T(1,128)} %get-tuple-element.11.loss, bf16[128,1536]{1,0:T(8,128)(2,1)} %get-tuple-element.12.hidden_grad, bf16[3,8,48,128]{3,2,1,0:T(8,128)(2,1)} %get-tuple-element.13.terms), custom_call_target="tpu_custom_call" | custom-call | tf_op jit(solution)/shard_map/finish/pallas_call | solution.py:639

commit v7 on v6

--- a/solution.py
+++ b/solution.py
@@ -71,6 +71,7 @@
     GX,
     GT,
     Wb,
+    hidden_rows,
     agbuf,
     final,
     lossb,
@@ -531,10 +532,12 @@
     GX[rows, :] = jnp.where(lent, jnp.where(keep, GT[0], zero), GX[rows, :])
     own_rows = jnp.concatenate([own_low, own_high], axis=0)
     for r in range(0, DS, 512):
-        out_hidden[:, r : r + 512] = (
+        hidden_rows[:, r : r + 512] = (
             lax.dot_general(own_rows, Wown[r : r + 512, :], nt, preferred_element_type=F32)
             + lax.dot_general(GX[...], Woth[r : r + 512, :], nt, preferred_element_type=F32)
         ).astype(BF)
+    kept = [pltpu.make_async_copy(hidden_rows, out_hidden, loc.at[5])]
+    kept[0].start()
 
     arrived(lossr.at[4], loss_r.at[2])
     loss_total = lossb[2] + lossr[4]
@@ -545,7 +548,10 @@
     for c in range(CHUNKS):
         arrived(spare, ag_r.at[c], core == goal)
         arrived(agbuf.at[c], ag_r.at[c], core != goal)
-        out_terms[c] = agbuf[c]
+        kept.append(pltpu.make_async_copy(agbuf.at[c], out_terms.at[c], loc.at[6 + c]))
+        kept[-1].start()
+    for copy in kept:
+        copy.wait()
 
     for copy, cond in pending:
         if cond is None:
@@ -584,6 +590,7 @@
         pltpu.VMEM((ROWS, SW), BF),
         pltpu.VMEM((2, TAIL, SW), BF),
         pltpu.VMEM((2, SLOTS, SLOTS), BF),
+        pltpu.VMEM((ROWS, DS), BF),
         pltpu.VMEM((CHUNKS, 8, 48, 128), BF),
         pltpu.VMEM((CHUNKS, 48, 128), BF),
         pltpu.VMEM((3, 8, 128), F32),
@@ -601,7 +608,7 @@
         scratch.append(pltpu.VMEM((15,) + UNIT, BF))
     dma = pltpu.SemaphoreType.DMA
     scratch += [
-        dma((5,)),
+        dma((9,)),
         dma((7,)),
         dma((12,)),
         dma((18,)),
@@ -621,7 +628,7 @@
             jax.ShapeDtypeStruct((CHUNKS, 8, 48, 128), BF),
         ),
         in_specs=[anywhere] * 6,
-        out_specs=(vmem, vmem, vmem),
+        out_specs=(vmem, anywhere, anywhere),
         scratch_shapes=scratch,
         compiler_params=pltpu.CompilerParams(
             collective_id=0, has_side_effects=True, vmem_limit_bytes=56 * 1024 * 1024

time: 43 us -> 43.4 us (level)
  no operation moved by 1% of the time
where the time goes in v7:
time: 43.4 us; the launch traced here: 43.2 us
  Pallas kernels  42.6 us (98%)
  between operations  0.64 us (1%)
    pallas_call x1, Pallas kernels, per_device(): pl.pallas_call(kernel, out_shape=(jax.ShapeDtypeStruct((1, 128), F32), ja...  40.5 us
    pallas_call x1, Pallas kernels, per_device(): pl.pallas_call(finish, out_shape=(jax.ShapeDtypeStruct((1,), F32), jax.Sh...  2.07 us

profile of v7, /device:TPU:1, one launch (start us, length us, event | category | flops | bytes accessed | tf_op | source)
XLA Modules:
  0.0 43.2 jit_solution(5003288390159211061)
XLA Ops:
  0.6 40.5 %relations.1 = (f32[1,128]{1,0:T(1,128)}, bf16[128,1536]{1,0:T(8,128)(2,1)}, bf16[3,8,48,128]{3,2,1,0:T(8,128)(2,1)}) custom-call(bf16[128,2048]{1,0:T(8,128)(2,1)} %bitcast.4, bf16[128,2048]{1,0:T(8,128)(2,1)} %bitcast.5, bf16[128,1536]{1,0:T(8,128)(2,1)} %bitcast.6, bf16[1536,768]{1,0:T(8,128)(2,1)} %wq.1, bf16[1536,768]{1,0:T(8,128)(2,1)} %wk.1, ...), custom_call_target="tpu_custom_call" | custom-call | tf_op jit(solution)/shard_map/relations/pallas_call | solution.py:623
  41.2 2.1 %finish.1 = (f32[1]{0:T(128)}, bf16[128,1536]{1,0:T(8,128)(2,1)}, f32[96,768]{1,0:T(8,128)}, f32[96,768]{1,0:T(8,128)}) custom-call(f32[1,128]{1,0:T(1,128)} %get-tuple-element.11.loss, bf16[128,1536]{1,0:T(8,128)(2,1)} %get-tuple-element.12.hidden_grad, bf16[3,8,48,128]{3,2,1,0:T(8,128)(2,1)} %get-tuple-element.13.terms), custom_call_target="tpu_custom_call" | custom-call | tf_op jit(solution)/shard_map/finish/pallas_call | solution.py:646
